TPU v7x, 32 devices: a whole 2x2x4 slice. The times are simulated.
32 devices in a mesh: stars: 32 (over z, y, x, core).
Axes of the slice: x: 2, y: 2, z: 4, core: 2. Of those that a mesh axis runs over, the one named last changes fastest.
Arguments:
- positions: float32 [3, 8192], P(None, 'stars')
- velocities: float32 [3, 8192], P(None, 'stars'), may hold values from -3 to 3
- accelerations: float32 [3, 8192], P(None, 'stars'), may hold values from -360 to 360
- jerk_values: float32 [3, 8192], P(None, 'stars'), may hold values from -120 to 120
- masses: float32 [8192], P('stars'), may hold values from 3.6621095e-05 to 0.00036621094
- star_level: int32 [8192], P('stars'), may hold values from 0 to 3, as said below
- list_fine: int32 [16], replicated, may hold values from 0 to 8191, as said below
- list_mid: int32 [32], replicated, may hold values from 0 to 8191, as said below
- list_all: int32 [112], replicated, may hold values from 0 to 8191, as said below
Outputs:
- final_positions: float32 [3, 8192], P(None, 'stars')
- final_velocities: float32 [3, 8192], P(None, 'stars')
- final_accelerations: float32 [3, 8192], P(None, 'stars')
- final_jerks: float32 [3, 8192], P(None, 'stars')
Inputs may be any that keep to these rules, and one draw needn't show every extreme that they name: `star_level`: exactly 16 stars have level 3, 16 level 2, 80 level 1, the rest level 0; the first and the last star have level 3. `list_fine`: the indices of the stars whose star_level is 3, ascending. `list_mid`: the indices of the stars whose star_level is 2 or 3, ascending. `list_all`: the indices of the stars whose star_level is 1, 2 or 3, ascending.
All inputs are finite; a program needn't handle non-finite values.
Results may differ from a plain program's by a relative error of at most 0.0003.
Values sent between devices are 32-bit elements; how exact they have to be, the bound alone decides.
No kernel may reach another device: no remote copies, remote signals or barrier semaphores. Data moves between devices by JAX's collectives and lax.ppermute only.
A program may use at most 64 MiB of HBM per device.

v0:
```python
import functools

import jax
import jax.numpy as jnp
from jax import lax
from jax.experimental import pallas as pl
from jax.experimental.pallas import tpu as pltpu
from jax.sharding import PartitionSpec as P

softening = 0.0001
unit = 1.0 / 128.0
lanes = 128
vmem = pl.BlockSpec(memory_space=pltpu.VMEM)
smem = pl.BlockSpec(memory_space=pltpu.SMEM)


def predict(place, motion, pull, change, elapse):
    moved = place + elapse * (motion + elapse * (0.5 * pull + elapse * change * (1.0 / 6.0)))
    sped = motion + elapse * (pull + 0.5 * elapse * change)
    return moved, sped


def correct(place, motion, pull, change, pull_new, change_new, elapse):
    square = elapse * elapse * (1.0 / 12.0)
    sped = motion + 0.5 * elapse * (pull + pull_new) + square * (change - change_new)
    moved = place + 0.5 * elapse * (motion + sped) + square * (pull - pull_new)
    return moved, sped


def pack_kernel(place, motion, pull, change, mass, level, out, *held):
    place_at, motion_at, pull_at, change_at, mass_at, level_at, arrived = held
    sources = (place, motion, pull, change, mass, level)
    copies = [
        pltpu.make_async_copy(source, target, arrived.at[index])
        for index, (source, target) in enumerate(zip(sources, held))
    ]
    for copy in copies:
        copy.start()
    for copy in copies:
        copy.wait()
    out[15:16, :] = jnp.zeros((1, out.shape[1]), jnp.float32)
    for part, ref in enumerate((place_at, motion_at, pull_at, change_at)):
        out[4 * part : 4 * part + 3, :] = ref[...]
    for half in range(2):
        row = slice(half, half + 1)
        at = slice(half * lanes, (half + 1) * lanes)
        out[3:4, at] = jnp.where(level_at[row, :] <= 1, mass_at[row, :], 0.0)
        out[7:8, at] = mass_at[row, :]
        out[11:12, at] = level_at[row, :].astype(jnp.float32)


def plan_kernel(own, fine, mid, every, listed):
    first = lax.axis_index("stars") * own
    count_fine, count_mid, count_all = fine.shape[0], mid.shape[0], every.shape[0]
    order = 2 + count_all

    def merge(index, seen):
        star = mid[index]
        listed[order + count_fine + index - seen] = star
        same = star == fine[jnp.minimum(seen, count_fine - 1)]
        return seen + same.astype(jnp.int32)

    lax.fori_loop(0, count_mid, merge, jnp.int32(0), unroll=8)

    def keep(source, start):
        def one(index, carry):
            listed[start + index] = source[index]
            return carry

        lax.fori_loop(0, source.shape[0], one, 0, unroll=8)

    keep(fine, order)
    keep(every, 2)

    def below(bound):
        found = jnp.int32(0)
        for bit in reversed(range(count_all.bit_length())):
            at = found + (1 << bit)
            less = (at <= count_all) & (every[jnp.minimum(at, count_all) - 1] < bound)
            found = jnp.where(less, at, found)
        return found

    low = below(first)
    listed[0] = low
    listed[1] = below(first + own) - low


def rounds_of(devices):
    bits = devices.bit_length() - 1
    assert devices == 1 << bits
    rounds = []
    high = bits
    while high > 1:
        width = 1 if high == 2 else 2
        high -= width
        rounds.append((1 << high, 1 << width))
    return rounds


def settle(value):
    return pl.pallas_call(
        lambda source, target: None,
        out_shape=jax.ShapeDtypeStruct(value.shape, value.dtype),
        in_specs=[pl.BlockSpec(memory_space=pl.ANY)],
        out_specs=pl.BlockSpec(memory_space=pl.ANY),
        input_output_aliases={0: 0},
        cost_estimate=pl.CostEstimate(flops=10**11, bytes_accessed=10**8, transcendentals=0),
        compiler_params=pltpu.CompilerParams(vmem_limit_bytes=1024 * 1024),
        name="settle",
    )(value)


def gather(block, devices, lists, plan):
    everyone = range(devices)
    odd = lax.axis_index("stars") % 2 == 1

    def fetch(value, even_by, odd_by):
        pairs = [(device, device ^ (odd_by if device % 2 else even_by)) for device in everyone]
        return lax.ppermute(value, "stars", pairs)

    def both(mine, other):
        return [jnp.where(odd, other, mine), jnp.where(odd, mine, other)]

    block = jnp.concatenate(both(block, fetch(block, 1, 1)), axis=0)
    rounds = rounds_of(devices)
    planned = None if rounds else plan(lists)
    for stride, radix in rounds:
        last = stride == rounds[-1][0]
        if last:
            block, lists = lax.optimization_barrier((block, lists))
            planned = plan(lists)
        if radix == 2:
            parts = [block, fetch(block, stride, stride)]
        elif last:
            half = block.shape[0] // 2
            one = fetch(block, stride, 2 * stride)
            two = jnp.where(odd, block[half:], block[:half])
            two = settle(fetch(two, 3 * stride, 3 * stride))
            parts = [block] + both(one, fetch(one, 1, 1)) + both(two, fetch(two, 1, 1))
        else:
            one = fetch(block, stride, 3 * stride)
            two = settle(fetch(block, 2 * stride, 2 * stride))
            near, far = both(one, fetch(one, 1, 1))
            parts = [block, near, two, far]
        block = jnp.concatenate(parts, axis=0)
    return block, planned


def slot_of(device, me, devices):
    slot, held = device % 2, 2
    for stride, radix in rounds_of(devices):
        slot = slot + (device ^ me) // stride % radix * held
        held *= radix
    return slot


def pair_terms(target, field, total):
    apart = [field[index] - target[index] for index in range(3)]
    closing = [field[3 + index] - target[3 + index] for index in range(3)]
    distance = apart[0] * apart[0] + apart[1] * apart[1] + (apart[2] * apart[2] + softening)
    inverse = lax.rsqrt(distance)
    square = inverse * inverse
    weight = field[6] * inverse * square
    dot = apart[0] * closing[0] + apart[1] * closing[1] + apart[2] * closing[2]
    rate = 3.0 * dot * square
    pulled = [weight * apart[index] for index in range(3)]
    return [total[index] + pulled[index] for index in range(3)] + [
        total[3 + index] + (weight * closing[index] - rate * pulled[index]) for index in range(3)
    ]


def main_kernel(
    devices,
    own_count,
    sizes,
    listed,
    field,
    out_place,
    out_motion,
    out_pull,
    out_change,
    ahead,
    slab,
    table,
    names,
    guess,
    mid_field,
    mid_state,
    mid_names,
    result,
):
    count_fine, count_mid, count_all = sizes
    blocks, blocks_fine = count_mid // 8, count_fine // 8
    groups = mid_field.shape[0]
    sub = lax.broadcasted_iota(jnp.int32, (8, lanes), 0)
    lane = lax.broadcasted_iota(jnp.int32, (8, lanes), 1)

    def spread(column):
        return jnp.broadcast_to(column, (8, lanes))

    def lane_total(value):
        return spread(jnp.sum(value, axis=1, keepdims=True))

    def loop(count, body):
        if count <= 4:
            for index in range(count):
                body(index)
        else:
            pl.loop(0, count)(body)

    def rows8(index):
        return pl.ds(index * 8 if isinstance(index, int) else pl.multiple_of(index * 8, 8), 8)

    halves = [slice(0, lanes), slice(lanes, 2 * lanes)]
    me = lax.axis_index("stars")
    first = me * own_count

    def look_ahead(index):
        for half in range(2):
            upper = field[pl.ds(pl.multiple_of(index * 16, 16), 8), halves[half]]
            lower = field[pl.ds(pl.multiple_of(index * 16 + 8, 8), 8), halves[half]]
            turned = pltpu.roll(lower, 4, 0)
            slope = jnp.where(sub < 4, pltpu.roll(upper, 4, 0), turned)
            bend = 0.5 * lower
            twist = jnp.where(sub < 4, turned * (1.0 / 6.0), 0.0)
            for step in range(4):
                time = (step + 1) * unit
                moved = upper + time * (slope + time * (bend + time * twist))
                ahead[step, index * 2 + half] = jnp.where(sub == 3, upper, moved)

    together = min(4, devices)

    @pl.loop(0, devices // together)
    def _(index):
        for inner in range(together):
            look_ahead(index * together + inner)

    low, count = listed[0], listed[1]

    mine = pl.multiple_of(slot_of(me, me, devices) * 16, 16)

    def own(part, component, half):
        tile = field[pl.ds(pl.multiple_of(mine + part // 2 * 8, 8), 8), halves[half]]
        at = part % 2 * 4 + component
        return tile[at : at + 1, :]

    def fetch(block):
        name = jnp.zeros((8, lanes), jnp.int32)
        for row in range(8):
            star = listed[2 + count_all + block * 8 + row]
            base = pl.multiple_of(slot_of(star // own_count, me, devices) * 16, 16)
            side = pl.multiple_of(star % own_count // lanes * lanes, lanes)
            slab[16 * row : 16 * row + 16, :] = field[pl.ds(base, 16), pl.ds(side, lanes)]
            name = jnp.where(sub == row, star, name)
        names[rows8(block), :] = name
        hit = (name % lanes) == lane
        for part in range(4):
            for component in range(3):
                value = slab[pl.ds(4 * part + component, 8, stride=16), :]
                table[3 * part + component, rows8(block), :] = lane_total(jnp.where(hit, value, 0.0))
        mass = slab[pl.ds(7, 8, stride=16), :]
        table[12, rows8(block), :] = lane_total(jnp.where(hit, mass, 0.0))

    loop(blocks, fetch)
    level = [own(2, 3, half) for half in range(2)]

    def turn(ref, group, *at):
        total = jnp.zeros((8, lanes), ref.dtype)
        for inner in range(min(16, blocks)):
            value = ref[(*at, rows8(group * 16 + inner), slice(None))]
            total = total + jnp.where(lane == sub + inner * 8, value, jnp.zeros_like(value))
        return jnp.sum(total, axis=0, keepdims=True)

    def fixed(group):
        mid_field[group, 6:7, :] = turn(table, group, 12)
        found = turn(names, group)
        if blocks * 8 < lanes:
            found = jnp.where(lane[0:1, :] < blocks * 8, found, -1)
        mid_names[group, 0:1, :] = found

    loop(groups, fixed)

    def elapse_of(step, fine):
        return unit * (1 if fine or step % 2 == 0 else 2)

    def guess_block(step, fine, block):
        state = [table[index, rows8(block), :] for index in range(12)]
        elapse = elapse_of(step, fine)
        for index in range(3):
            moved, sped = predict(
                state[index], state[3 + index], state[6 + index], state[9 + index], elapse
            )
            guess[index, rows8(block), :] = moved
            guess[3 + index, rows8(block), :] = sped

    def place_mid(group):
        for index in range(6):
            mid_field[group, index : index + 1, :] = turn(guess, group, index)

    def force(step, targets):
        def add(totals, row):
            return [pair_terms(target, row, total) for target, total in zip(targets, totals)]

        def one(index, totals):
            for half in range(2):
                row = [ahead[step, index * 2 + half, k : k + 1, :] for k in (0, 1, 2, 4, 5, 6, 3)]
                totals = add(totals, row)
            return totals

        together = min(8, devices)

        def some(index, totals):
            for inner in range(together):
                totals = one(index * together + inner, totals)
            return totals

        zero = jnp.zeros((8, lanes), jnp.float32)
        totals = [[zero] * 6 for _ in targets]
        for group in range(groups):
            totals = add(totals, [mid_field[group, k : k + 1, :] for k in range(7)])
        totals = lax.fori_loop(0, devices // together, some, totals)
        return [[lane_total(value) for value in total] for total in totals]

    for step in range(4):
        loop(blocks_fine, functools.partial(guess_block, step, True))
        loop(blocks - blocks_fine, lambda block: guess_block(step, False, block + blocks_fine))
        loop(groups, place_mid)
        if step == 3:
            break

        def advance(pair, step, fine):
            targets = [
                [guess[index, rows8(2 * pair + side), :] for index in range(6)] for side in range(2)
            ]
            elapse = elapse_of(step, fine)
            for side, total in enumerate(force(step, targets)):
                rows = rows8(2 * pair + side)
                for index in range(3):
                    moved, sped = correct(
                        *[table[3 * part + index, rows, :] for part in range(4)],
                        total[index],
                        total[3 + index],
                        elapse,
                    )
                    table[index, rows, :] = moved
                    table[3 + index, rows, :] = sped
                    table[6 + index, rows, :] = total[index]
                    table[9 + index, rows, :] = total[3 + index]

        loop(blocks_fine // 2, functools.partial(advance, step=step, fine=True))
        if step == 1:
            loop(
                (blocks - blocks_fine) // 2,
                lambda pair: advance(pair + blocks_fine // 2, step=1, fine=False),
            )

    def keep(group):
        for index in range(12):
            mid_state[group, index : index + 1, :] = turn(table, group, index)

    loop(groups, keep)
    result[...] = jnp.zeros_like(result)

    def finish(wide, turn_at):
        hits, states, elapses, targets = [], [], [], []
        for side in range(wide):
            name = jnp.full((8, lanes), -1, jnp.int32)
            for row in range(8):
                at = (turn_at * wide + side) * 8 + row
                star = listed[2 + jnp.minimum(low + at, count_all - 1)]
                name = jnp.where((sub == row) & (at < count), star, name)
            own_hit = [name == lane + (first + half * lanes) for half in range(2)]
            coarse = [own_hit[half] & (level[half] == 1.0) for half in range(2)]
            mid_hit = [name == mid_names[group, 0:1, :] for group in range(groups)]

            def find(part, component):
                total = jnp.zeros((8, lanes), jnp.float32)
                for half in range(2):
                    total = jnp.where(coarse[half], own(part, component, half), total)
                for group in range(groups):
                    at = 3 * part + component
                    total = jnp.where(mid_hit[group], mid_state[group, at : at + 1, :], total)
                return lane_total(total)

            total = jnp.zeros((8, lanes), jnp.float32)
            for half in range(2):
                total = jnp.where(coarse[half], 4 * unit, total)
            for group in range(groups):
                fine = jnp.where(lane + group * lanes < count_fine, unit, 2 * unit)
                total = jnp.where(mid_hit[group], fine, total)
            elapse = lane_total(total)
            state = [[find(part, index) for index in range(3)] for part in range(4)]
            pairs = [
                predict(*[state[part][index] for part in range(4)], elapse) for index in range(3)
            ]
            hits.append(own_hit)
            states.append(state)
            elapses.append(elapse)
            targets.append([pair[0] for pair in pairs] + [pair[1] for pair in pairs])
        for side, total in enumerate(force(3, targets)):
            for index in range(3):
                moved, sped = correct(
                    *[states[side][part][index] for part in range(4)],
                    total[index],
                    total[3 + index],
                    elapses[side],
                )
                for part, value in enumerate((moved, sped, total[index], total[3 + index])):
                    for half in range(2):
                        result[part, half, index] += jnp.where(hits[side][half], value, 0.0)

    @pl.when((count > 0) & (count <= 16))
    def _():
        finish(2, 0)

    @pl.when(count > 16)
    def _():
        pl.loop(0, (count + 23) // 24)(functools.partial(finish, 3))

    for part, ref in enumerate((out_place, out_motion, out_pull, out_change)):
        for half in range(2):
            changed = level[half] >= 1.0
            for index in range(3):
                value = jnp.sum(result[part, half, index], axis=0, keepdims=True)
                ref[index : index + 1, halves[half]] = jnp.where(
                    changed, value, own(part, index, half)
                )


def body(devices, place, motion, pull, change, masses, star_level, fine, mid, every):
    own_count = place.shape[1]
    sizes = (fine.shape[0], mid.shape[0], every.shape[0])
    groups = -(-sizes[1] // lanes)
    held = [pltpu.VMEM((3, own_count), jnp.float32)] * 4
    held += [pltpu.VMEM((2, lanes), jnp.float32), pltpu.VMEM((2, lanes), jnp.int32)]
    block = pl.pallas_call(
        pack_kernel,
        out_shape=jax.ShapeDtypeStruct((16, own_count), jnp.float32),
        in_specs=[pl.BlockSpec(memory_space=pl.ANY)] * 6,
        out_specs=vmem,
        scratch_shapes=held + [pltpu.SemaphoreType.DMA((6,))],
        name="pack",
    )(place, motion, pull, change, masses.reshape(2, lanes), star_level.reshape(2, lanes))

    def plan(lists):
        return pl.pallas_call(
            functools.partial(plan_kernel, own_count),
            out_shape=jax.ShapeDtypeStruct((2 + sizes[2] + sizes[1] + 6,), jnp.int32),
            in_specs=[smem] * 3,
            out_specs=smem,
            compiler_params=pltpu.CompilerParams(vmem_limit_bytes=1024 * 1024),
            name="plan",
        )(*lists)

    whole, listed = gather(block, devices, (fine, mid, every), plan)
    room = devices * 52 * 1024 + sizes[1] * 12 * 1024 + 3 * 1024 * 1024
    result = jax.ShapeDtypeStruct((3, own_count), jnp.float32)
    return pl.pallas_call(
        functools.partial(main_kernel, devices, own_count, sizes),
        out_shape=(result,) * 4,
        in_specs=[smem, vmem],
        out_specs=(vmem,) * 4,
        scratch_shapes=[
            pltpu.VMEM((4, devices * 2, 8, lanes), jnp.float32),
            pltpu.VMEM((8 * 16, lanes), jnp.float32),
            pltpu.VMEM((13, sizes[1], lanes), jnp.float32),
            pltpu.VMEM((sizes[1], lanes), jnp.int32),
            pltpu.VMEM((6, sizes[1], lanes), jnp.float32),
            pltpu.VMEM((groups, 8, lanes), jnp.float32),
            pltpu.VMEM((groups, 16, lanes), jnp.float32),
            pltpu.VMEM((groups, 8, lanes), jnp.int32),
            pltpu.VMEM((4, 2, 3, 8, lanes), jnp.float32),
        ],
        compiler_params=pltpu.CompilerParams(vmem_limit_bytes=room),
        name="steps",
    )(listed, whole)


def solution(mesh):
    split = P(None, "stars")
    return jax.shard_map(
        functools.partial(body, mesh.shape["stars"]),
        mesh=mesh,
        in_specs=(split,) * 4 + (P("stars"),) * 2 + (P(),) * 3,
        out_specs=(split,) * 4,
        check_vma=False,
    )
```

profile of v0, /device:TPU:0, one launch (start us, length us, event | category | flops | bytes accessed | tf_op | source)
XLA Modules:
  0.0 28.1 jit_solution(557457216445679315)
XLA Ops:
  0.6 1.4 %pack.1 = f32[16,256]{1,0:T(8,128)} custom-call(f32[3,256]{1,0:T(4,128)} %place.1, f32[3,256]{1,0:T(4,128)} %motion.1, f32[3,256]{1,0:T(4,128)} %pull.1, f32[3,256]{1,0:T(4,128)} %change.1, f32[2,128]{1,0:T(2,128)} %bitcast.2, s32[2,128]{1,0:T(2,128)} %bitcast.3), custom_call_target="tpu_custom_call" | custom-call | tf_op jit(solution)/shard_map/pack/pallas_call | solution.py:436
  2.1 0.0 copy-start.3
  2.1 0.5 %collective-permute-start = (f32[16,256]{1,0:T(8,128)}, f32[16,256]{1,0:T(8,128)S(1)}, u32[]{:S(2)}, u32[]{:S(2)}) collective-permute-start(f32[16,256]{1,0:T(8,128)} %pack.1), channel_id=1, source_target_pairs={{0,1},{1,0},{2,3},{3,2},{4,5},{5,4},{6,7},{7,6},{8,9},{9,8},{10,11... | collective-permute-start | bytes 49160 | tf_op jit(solution)/shard_map/ppermute | solution.py:119
  2.6 1.0 %collective-permute-done = f32[16,256]{1,0:T(8,128)S(1)} collective-permute-done((f32[16,256]{1,0:T(8,128)}, f32[16,256]{1,0:T(8,128)S(1)}, u32[]{:S(2)}, u32[]{:S(2)}) %collective-permute-start) | collective-permute-done | bytes 16416 | tf_op jit(solution)/shard_map/ppermute | solution.py:119
  3.6 0.0 copy-done.3
  3.7 3.0 %collective-permute-start.1 = (f32[32,256]{1,0:T(8,128)S(1)}, f32[32,256]{1,0:T(8,128)S(1)}, u32[]{:S(2)}, u32[]{:S(2)}) collective-permute-start(f32[32,256]{1,0:T(8,128)S(1)} %pad_maximum_fusion), channel_id=1, source_target_pairs={{0,8},{1,25},{2,10},{3,27},{4,12},{5,29},{6,14},{7,31},{8,0},{9,17... | collective-permute-start | bytes 98312 | tf_op jit(solution)/shard_map/ppermute | solution.py:119
  6.7 2.6 %collective-permute-start.3 = (f32[32,256]{1,0:T(8,128)S(1)}, f32[32,256]{1,0:T(8,128)S(1)}, u32[]{:S(2)}, u32[]{:S(2)}) collective-permute-start(f32[32,256]{1,0:T(8,128)S(1)} %pad_maximum_fusion), channel_id=1, source_target_pairs={{0,16},{1,17},{2,18},{3,19},{4,20},{5,21},{6,22},{7,23},{8,24},{9,... | collective-permute-start | bytes 98312 | tf_op jit(solution)/shard_map/ppermute | solution.py:119
  9.3 0.0 collective-permute-done.1
  9.3 0.6 %collective-permute-start.2 = (f32[32,256]{1,0:T(8,128)S(1)}, f32[32,256]{1,0:T(8,128)S(1)}, u32[]{:S(2)}, u32[]{:S(2)}) collective-permute-start(f32[32,256]{1,0:T(8,128)S(1)} %collective-permute-done.1), channel_id=1, source_target_pairs={{0,1},{1,0},{2,3},{3,2},{4,5},{5,4},{6,7},{7,6},{8,9},{9,8},{10,11... | collective-permute-start | bytes 98312 | tf_op jit(solution)/shard_map/ppermute | solution.py:119
  9.9 2.2 %collective-permute-done.3.source = f32[32,256]{1,0:T(8,128)S(1)} collective-permute-done((f32[32,256]{1,0:T(8,128)S(1)}, f32[32,256]{1,0:T(8,128)S(1)}, u32[]{:S(2)}, u32[]{:S(2)}) %collective-permute-start.3) | collective-permute-done | bytes 32800 | tf_op jit(solution)/shard_map/ppermute | solution.py:119
  12.1 0.0 collective-permute-done.2
  12.1 0.0 copy-start
  12.1 0.0 copy-start.1
  12.2 0.0 copy-start.2
  12.2 1.6 %collective-permute-start.4 = (f32[128,256]{1,0:T(8,128)S(1)}, f32[128,256]{1,0:T(8,128)S(1)}, u32[]{:S(2)}, u32[]{:S(2)}) collective-permute-start(f32[128,256]{1,0:T(8,128)S(1)} %select_dynamic-update-slice_fusion.4), channel_id=1, source_target_pairs={{0,2},{1,5},{2,0},{3,7},{4,6},{5,1},{6,4},{7,3},{8,10},{9,13},{10,... | collective-permute-start | bytes 393224 | tf_op jit(solution)/shard_map/ppermute | solution.py:119
  13.7 1.6 %collective-permute-start.6 = (f32[64,256]{1,0:T(8,128)S(1)}, f32[64,256]{1,0:T(8,128)S(1)}, u32[]{:S(2)}, u32[]{:S(2)}) collective-permute-start(f32[64,256]{1,0:T(8,128)S(1)} %slice_select_fusion), channel_id=1, source_target_pairs={{0,6},{1,7},{2,4},{3,5},{4,2},{5,3},{6,0},{7,1},{8,14},{9,15},{10,... | collective-permute-start | bytes 196616 | tf_op jit(solution)/shard_map/ppermute | solution.py:119
  15.3 0.0 copy-done
  15.3 0.0 copy-done.1
  15.3 0.0 copy-done.2
  15.3 1.7 %plan.1.listed = s32[152]{0:T(256)S(1)} custom-call(s32[16]{0:T(128)S(1)} %copy-done, s32[32]{0:T(128)S(1)} %copy-done.1, s32[112]{0:T(128)S(1)} %copy-done.2), custom_call_target="tpu_custom_call" | custom-call | tf_op jit(solution)/shard_map/plan/pallas_call | solution.py:446
  17.0 0.9 %collective-permute-done.4 = f32[128,256]{1,0:T(8,128)S(1)} collective-permute-done((f32[128,256]{1,0:T(8,128)S(1)}, f32[128,256]{1,0:T(8,128)S(1)}, u32[]{:S(2)}, u32[]{:S(2)}) %collective-permute-start.4) | collective-permute-done | bytes 131104 | tf_op jit(solution)/shard_map/ppermute | solution.py:119
  17.9 0.0 collective-permute-start.5
  17.9 1.7 %collective-permute-done.6.source = f32[64,256]{1,0:T(8,128)S(1)} collective-permute-done((f32[64,256]{1,0:T(8,128)S(1)}, f32[64,256]{1,0:T(8,128)S(1)}, u32[]{:S(2)}, u32[]{:S(2)}) %collective-permute-start.6) | collective-permute-done | bytes 65568 | tf_op jit(solution)/shard_map/ppermute | solution.py:119
  19.6 0.0 collective-permute-start.7
  19.6 0.0 collective-permute-done.5
  19.6 1.2 %collective-permute-done.7 = f32[64,256]{1,0:T(8,128)S(1)} collective-permute-done((f32[64,256]{1,0:T(8,128)S(1)}, f32[64,256]{1,0:T(8,128)S(1)}, u32[]{:S(2)}, u32[]{:S(2)}) %collective-permute-start.7) | collective-permute-done | bytes 65568 | tf_op jit(solution)/shard_map/ppermute | solution.py:119
  20.9 7.2 %steps.1 = (f32[3,256]{1,0:T(4,128)}, f32[3,256]{1,0:T(4,128)}, f32[3,256]{1,0:T(4,128)}, f32[3,256]{1,0:T(4,128)}) custom-call(s32[152]{0:T(256)S(1)} %plan.1.listed, f32[512,256]{1,0:T(8,128)S(1)} %select_dynamic-update-slice_fusion.2.field), custom_call_target="tpu_custom_call" | custom-call | tf_op jit(solution)/shard_map/steps/pallas_call | solution.py:458
  (14 shorter events, 0.1 us)
Async XLA Ops:
  2.1 1.6 %copy-start.3 = (f32[16,256]{1,0:T(8,128)S(1)}, f32[16,256]{1,0:T(8,128)}, u32[]{:S(2)}) copy-start(f32[16,256]{1,0:T(8,128)} %pack.1) | copy-start | bytes 49156
  2.1 1.6 %collective-permute-start = (f32[16,256]{1,0:T(8,128)}, f32[16,256]{1,0:T(8,128)S(1)}, u32[]{:S(2)}, u32[]{:S(2)}) collective-permute-start(f32[16,256]{1,0:T(8,128)} %pack.1), channel_id=1, source_target_pairs={{0,1},{1,0},{2,3},{3,2},{4,5},{5,4},{6,7},{7,6},{8,9},{9,8},{10,11... | collective-permute-start | bytes 49160 | tf_op jit(solution)/shard_map/ppermute | solution.py:119
  3.7 5.6 %collective-permute-start.1 = (f32[32,256]{1,0:T(8,128)S(1)}, f32[32,256]{1,0:T(8,128)S(1)}, u32[]{:S(2)}, u32[]{:S(2)}) collective-permute-start(f32[32,256]{1,0:T(8,128)S(1)} %pad_maximum_fusion), channel_id=1, source_target_pairs={{0,8},{1,25},{2,10},{3,27},{4,12},{5,29},{6,14},{7,31},{8,0},{9,17... | collective-permute-start | bytes 98312 | tf_op jit(solution)/shard_map/ppermute | solution.py:119
  6.7 5.4 %collective-permute-start.3 = (f32[32,256]{1,0:T(8,128)S(1)}, f32[32,256]{1,0:T(8,128)S(1)}, u32[]{:S(2)}, u32[]{:S(2)}) collective-permute-start(f32[32,256]{1,0:T(8,128)S(1)} %pad_maximum_fusion), channel_id=1, source_target_pairs={{0,16},{1,17},{2,18},{3,19},{4,20},{5,21},{6,22},{7,23},{8,24},{9,... | collective-permute-start | bytes 98312 | tf_op jit(solution)/shard_map/ppermute | solution.py:119
  9.3 2.8 %collective-permute-start.2 = (f32[32,256]{1,0:T(8,128)S(1)}, f32[32,256]{1,0:T(8,128)S(1)}, u32[]{:S(2)}, u32[]{:S(2)}) collective-permute-start(f32[32,256]{1,0:T(8,128)S(1)} %collective-permute-done.1), channel_id=1, source_target_pairs={{0,1},{1,0},{2,3},{3,2},{4,5},{5,4},{6,7},{7,6},{8,9},{9,8},{10,11... | collective-permute-start | bytes 98312 | tf_op jit(solution)/shard_map/ppermute | solution.py:119
  12.1 3.2 %copy-start = (s32[16]{0:T(128)S(1)}, s32[16]{0:T(128)}, u32[]{:S(2)}) copy-start(s32[16]{0:T(128)} %fine) | copy-start | bytes 196
  12.1 3.2 %copy-start.1 = (s32[32]{0:T(128)S(1)}, s32[32]{0:T(128)}, u32[]{:S(2)}) copy-start(s32[32]{0:T(128)} %mid) | copy-start | bytes 388
  12.2 3.1 %copy-start.2 = (s32[112]{0:T(128)S(1)}, s32[112]{0:T(128)}, u32[]{:S(2)}) copy-start(s32[112]{0:T(128)} %every) | copy-start | bytes 1348
  12.2 5.7 %collective-permute-start.4 = (f32[128,256]{1,0:T(8,128)S(1)}, f32[128,256]{1,0:T(8,128)S(1)}, u32[]{:S(2)}, u32[]{:S(2)}) collective-permute-start(f32[128,256]{1,0:T(8,128)S(1)} %select_dynamic-update-slice_fusion.4), channel_id=1, source_target_pairs={{0,2},{1,5},{2,0},{3,7},{4,6},{5,1},{6,4},{7,3},{8,10},{9,13},{10,... | collective-permute-start | bytes 393224 | tf_op jit(solution)/shard_map/ppermute | solution.py:119
  13.7 5.8 %collective-permute-start.6 = (f32[64,256]{1,0:T(8,128)S(1)}, f32[64,256]{1,0:T(8,128)S(1)}, u32[]{:S(2)}, u32[]{:S(2)}) collective-permute-start(f32[64,256]{1,0:T(8,128)S(1)} %slice_select_fusion), channel_id=1, source_target_pairs={{0,6},{1,7},{2,4},{3,5},{4,2},{5,3},{6,0},{7,1},{8,14},{9,15},{10,... | collective-permute-start | bytes 196616 | tf_op jit(solution)/shard_map/ppermute | solution.py:119
  17.9 1.7 %collective-permute-start.5 = (f32[128,256]{1,0:T(8,128)S(1)}, f32[128,256]{1,0:T(8,128)S(1)}, u32[]{:S(2)}, u32[]{:S(2)}) collective-permute-start(f32[128,256]{1,0:T(8,128)S(1)} %collective-permute-done.4), channel_id=1, source_target_pairs={{0,1},{1,0},{2,3},{3,2},{4,5},{5,4},{6,7},{7,6},{8,9},{9,8},{10,11... | collective-permute-start | bytes 393224 | tf_op jit(solution)/shard_map/ppermute | solution.py:119
  19.6 1.3 %collective-permute-start.7 = (f32[64,256]{1,0:T(8,128)S(1)}, f32[64,256]{1,0:T(8,128)S(1)}, u32[]{:S(2)}, u32[]{:S(2)}) collective-permute-start(f32[64,256]{1,0:T(8,128)S(1)} %settle.3), channel_id=1, source_target_pairs={{0,1},{1,0},{2,3},{3,2},{4,5},{5,4},{6,7},{7,6},{8,9},{9,8},{10,11... | collective-permute-start | bytes 196616 | tf_op jit(solution)/shard_map/ppermute | solution.py:119
where the time goes:
time: 28.3 us; the launch traced here: 28.1 us
  Pallas kernels  10.3 us (36%)
  starting transfers between devices  9.83 us (35%)
  waiting for transfers between devices  7.04 us (25%)
  between operations  0.76 us (3%)
    ppermute x8, starting transfers between devices, fetch(): return lax.ppermute(value, 'stars', pairs)  9.83 us
    pallas_call x1, Pallas kernels, body(): pl.pallas_call(functools.partial(main_kernel, devices, own_count, sizes),...  7.23 us
    ppermute x8, waiting for transfers between devices, fetch(): return lax.ppermute(value, 'stars', pairs)  7.04 us
    pallas_call x1, Pallas kernels, plan(): pl.pallas_call(functools.partial(plan_kernel, own_count), out_shape=jax.S...  1.67 us
    pallas_call x1, Pallas kernels, body(): pl.pallas_call(pack_kernel, out_shape=jax.ShapeDtypeStruct((16, own_count...  1.42 us
  transfers between devices with their start and end apart: 8, of which 5 were waited for; matrix products, arithmetic and copies ran while one was open for 0% of the time, Pallas kernels for 6%

commit v1 on v0

--- a/solution.py
+++ b/solution.py
@@ -138,10 +138,9 @@
             two = settle(fetch(two, 3 * stride, 3 * stride))
             parts = [block] + both(one, fetch(one, 1, 1)) + both(two, fetch(two, 1, 1))
         else:
-            one = fetch(block, stride, 3 * stride)
-            two = settle(fetch(block, 2 * stride, 2 * stride))
-            near, far = both(one, fetch(one, 1, 1))
-            parts = [block, near, two, far]
+            one = fetch(block, 2 * stride, 3 * stride)
+            near = settle(fetch(block, stride, stride))
+            parts = [block, near] + both(one, fetch(one, 1, 1))
         block = jnp.concatenate(parts, axis=0)
     return block, planned
 

time: 28.3 us -> 29.2 us (1.032)
  waiting for transfers between devices: 7.04 us -> 8.84 us
  starting transfers between devices: 9.83 us -> 9.22 us
    ppermute x8, waiting for transfers between devices: 7.04 us -> 8.84 us  [fetch(): return lax.ppermute(value, 'stars', pairs)]
    ppermute x8, starting transfers between devices: 9.83 us -> 9.22 us  [fetch(): return lax.ppermute(value, 'stars', pairs)]
  transfers between devices with their start and end apart: 8 -> 8, of which waited for: 5 -> 6; matrix products, arithmetic and copies ran while one was open for 0% -> 0% of each run, Pallas kernels for 6% -> 6%
where the time goes in v1:
time: 29.2 us; the launch traced here: 29.3 us
  Pallas kernels  10.3 us (35%)
  starting transfers between devices  9.22 us (32%)
  waiting for transfers between devices  8.84 us (30%)
  between operations  0.74 us (3%)
    ppermute x8, starting transfers between devices, fetch(): return lax.ppermute(value, 'stars', pairs)  9.22 us
    ppermute x8, waiting for transfers between devices, fetch(): return lax.ppermute(value, 'stars', pairs)  8.84 us
    pallas_call x1, Pallas kernels, body(): pl.pallas_call(functools.partial(main_kernel, devices, own_count, sizes),...  7.23 us
    pallas_call x1, Pallas kernels, plan(): pl.pallas_call(functools.partial(plan_kernel, own_count), out_shape=jax.S...  1.67 us
    pallas_call x1, Pallas kernels, body(): pl.pallas_call(pack_kernel, out_shape=jax.ShapeDtypeStruct((16, own_count...  1.42 us
  transfers between devices with their start and end apart: 8, of which 6 were waited for; matrix products, arithmetic and copies ran while one was open for 0% of the time, Pallas kernels for 6%

profile of v1, /device:TPU:0, one launch (start us, length us, event | category | flops | bytes accessed | tf_op | source)
XLA Modules:
  0.0 29.3 jit_solution(7213930805839088343)
XLA Ops:
  0.6 1.4 %pack.1 = f32[16,256]{1,0:T(8,128)} custom-call(f32[3,256]{1,0:T(4,128)} %place.1, f32[3,256]{1,0:T(4,128)} %motion.1, f32[3,256]{1,0:T(4,128)} %pull.1, f32[3,256]{1,0:T(4,128)} %change.1, f32[2,128]{1,0:T(2,128)} %bitcast.2, s32[2,128]{1,0:T(2,128)} %bitcast.3), custom_call_target="tpu_custom_call" | custom-call | tf_op jit(solution)/shard_map/pack/pallas_call | solution.py:435
  2.1 0.0 copy-start.3
  2.1 0.5 %collective-permute-start = (f32[16,256]{1,0:T(8,128)}, f32[16,256]{1,0:T(8,128)S(1)}, u32[]{:S(2)}, u32[]{:S(2)}) collective-permute-start(f32[16,256]{1,0:T(8,128)} %pack.1), channel_id=1, source_target_pairs={{0,1},{1,0},{2,3},{3,2},{4,5},{5,4},{6,7},{7,6},{8,9},{9,8},{10,11... | collective-permute-start | bytes 49160 | tf_op jit(solution)/shard_map/ppermute | solution.py:119
  2.6 1.0 %collective-permute-done = f32[16,256]{1,0:T(8,128)S(1)} collective-permute-done((f32[16,256]{1,0:T(8,128)}, f32[16,256]{1,0:T(8,128)S(1)}, u32[]{:S(2)}, u32[]{:S(2)}) %collective-permute-start) | collective-permute-done | bytes 16416 | tf_op jit(solution)/shard_map/ppermute | solution.py:119
  3.6 0.0 copy-done.3
  3.7 3.0 %collective-permute-start.1 = (f32[32,256]{1,0:T(8,128)S(1)}, f32[32,256]{1,0:T(8,128)S(1)}, u32[]{:S(2)}, u32[]{:S(2)}) collective-permute-start(f32[32,256]{1,0:T(8,128)S(1)} %pad_maximum_fusion), channel_id=1, source_target_pairs={{0,8},{1,9},{2,10},{3,11},{4,12},{5,13},{6,14},{7,15},{8,0},{9,1},... | collective-permute-start | bytes 98312 | tf_op jit(solution)/shard_map/ppermute | solution.py:119
  6.7 2.6 %collective-permute-start.2 = (f32[32,256]{1,0:T(8,128)S(1)}, f32[32,256]{1,0:T(8,128)S(1)}, u32[]{:S(2)}, u32[]{:S(2)}) collective-permute-start(f32[32,256]{1,0:T(8,128)S(1)} %pad_maximum_fusion), channel_id=1, source_target_pairs={{0,16},{1,25},{2,18},{3,27},{4,20},{5,29},{6,22},{7,31},{8,24},{9,... | collective-permute-start | bytes 98312 | tf_op jit(solution)/shard_map/ppermute | solution.py:119
  9.3 0.0 collective-permute-done.1.source
  9.3 2.8 %collective-permute-done.2 = f32[32,256]{1,0:T(8,128)S(1)} collective-permute-done((f32[32,256]{1,0:T(8,128)S(1)}, f32[32,256]{1,0:T(8,128)S(1)}, u32[]{:S(2)}, u32[]{:S(2)}) %collective-permute-start.2) | collective-permute-done | bytes 32800 | tf_op jit(solution)/shard_map/ppermute | solution.py:119
  12.1 0.0 collective-permute-start.3
  12.1 1.2 %collective-permute-done.3 = f32[32,256]{1,0:T(8,128)S(1)} collective-permute-done((f32[32,256]{1,0:T(8,128)S(1)}, f32[32,256]{1,0:T(8,128)S(1)}, u32[]{:S(2)}, u32[]{:S(2)}) %collective-permute-start.3) | collective-permute-done | bytes 32800 | tf_op jit(solution)/shard_map/ppermute | solution.py:119
  13.3 0.0 copy-start
  13.3 0.0 copy-start.1
  13.3 0.0 copy-start.2
  13.3 1.6 %collective-permute-start.4 = (f32[128,256]{1,0:T(8,128)S(1)}, f32[128,256]{1,0:T(8,128)S(1)}, u32[]{:S(2)}, u32[]{:S(2)}) collective-permute-start(f32[128,256]{1,0:T(8,128)S(1)} %select_dynamic-update-slice_fusion.4), channel_id=1, source_target_pairs={{0,2},{1,5},{2,0},{3,7},{4,6},{5,1},{6,4},{7,3},{8,10},{9,13},{10,... | collective-permute-start | bytes 393224 | tf_op jit(solution)/shard_map/ppermute | solution.py:119
  14.9 1.6 %collective-permute-start.6 = (f32[64,256]{1,0:T(8,128)S(1)}, f32[64,256]{1,0:T(8,128)S(1)}, u32[]{:S(2)}, u32[]{:S(2)}) collective-permute-start(f32[64,256]{1,0:T(8,128)S(1)} %slice_select_fusion), channel_id=1, source_target_pairs={{0,6},{1,7},{2,4},{3,5},{4,2},{5,3},{6,0},{7,1},{8,14},{9,15},{10,... | collective-permute-start | bytes 196616 | tf_op jit(solution)/shard_map/ppermute | solution.py:119
  16.5 0.0 copy-done
  16.5 0.0 copy-done.1
  16.5 0.0 copy-done.2
  16.5 1.7 %plan.1.listed = s32[152]{0:T(256)S(1)} custom-call(s32[16]{0:T(128)S(1)} %copy-done, s32[32]{0:T(128)S(1)} %copy-done.1, s32[112]{0:T(128)S(1)} %copy-done.2), custom_call_target="tpu_custom_call" | custom-call | tf_op jit(solution)/shard_map/plan/pallas_call | solution.py:445
  18.2 0.9 %collective-permute-done.4 = f32[128,256]{1,0:T(8,128)S(1)} collective-permute-done((f32[128,256]{1,0:T(8,128)S(1)}, f32[128,256]{1,0:T(8,128)S(1)}, u32[]{:S(2)}, u32[]{:S(2)}) %collective-permute-start.4) | collective-permute-done | bytes 131104 | tf_op jit(solution)/shard_map/ppermute | solution.py:119
  19.1 0.0 collective-permute-start.5
  19.1 1.7 %collective-permute-done.6.source = f32[64,256]{1,0:T(8,128)S(1)} collective-permute-done((f32[64,256]{1,0:T(8,128)S(1)}, f32[64,256]{1,0:T(8,128)S(1)}, u32[]{:S(2)}, u32[]{:S(2)}) %collective-permute-start.6) | collective-permute-done | bytes 65568 | tf_op jit(solution)/shard_map/ppermute | solution.py:119
  20.7 0.0 collective-permute-start.7
  20.7 0.0 collective-permute-done.5
  20.8 1.2 %collective-permute-done.7 = f32[64,256]{1,0:T(8,128)S(1)} collective-permute-done((f32[64,256]{1,0:T(8,128)S(1)}, f32[64,256]{1,0:T(8,128)S(1)}, u32[]{:S(2)}, u32[]{:S(2)}) %collective-permute-start.7) | collective-permute-done | bytes 65568 | tf_op jit(solution)/shard_map/ppermute | solution.py:119
  22.0 7.2 %steps.1 = (f32[3,256]{1,0:T(4,128)}, f32[3,256]{1,0:T(4,128)}, f32[3,256]{1,0:T(4,128)}, f32[3,256]{1,0:T(4,128)}) custom-call(s32[152]{0:T(256)S(1)} %plan.1.listed, f32[512,256]{1,0:T(8,128)S(1)} %select_dynamic-update-slice_fusion.2.field), custom_call_target="tpu_custom_call" | custom-call | tf_op jit(solution)/shard_map/steps/pallas_call | solution.py:457
  (14 shorter events, 0.1 us)
Async XLA Ops:
  2.1 1.6 %copy-start.3 = (f32[16,256]{1,0:T(8,128)S(1)}, f32[16,256]{1,0:T(8,128)}, u32[]{:S(2)}) copy-start(f32[16,256]{1,0:T(8,128)} %pack.1) | copy-start | bytes 49156
  2.1 1.6 %collective-permute-start = (f32[16,256]{1,0:T(8,128)}, f32[16,256]{1,0:T(8,128)S(1)}, u32[]{:S(2)}, u32[]{:S(2)}) collective-permute-start(f32[16,256]{1,0:T(8,128)} %pack.1), channel_id=1, source_target_pairs={{0,1},{1,0},{2,3},{3,2},{4,5},{5,4},{6,7},{7,6},{8,9},{9,8},{10,11... | collective-permute-start | bytes 49160 | tf_op jit(solution)/shard_map/ppermute | solution.py:119
  3.7 5.6 %collective-permute-start.1 = (f32[32,256]{1,0:T(8,128)S(1)}, f32[32,256]{1,0:T(8,128)S(1)}, u32[]{:S(2)}, u32[]{:S(2)}) collective-permute-start(f32[32,256]{1,0:T(8,128)S(1)} %pad_maximum_fusion), channel_id=1, source_target_pairs={{0,8},{1,9},{2,10},{3,11},{4,12},{5,13},{6,14},{7,15},{8,0},{9,1},... | collective-permute-start | bytes 98312 | tf_op jit(solution)/shard_map/ppermute | solution.py:119
  6.7 5.4 %collective-permute-start.2 = (f32[32,256]{1,0:T(8,128)S(1)}, f32[32,256]{1,0:T(8,128)S(1)}, u32[]{:S(2)}, u32[]{:S(2)}) collective-permute-start(f32[32,256]{1,0:T(8,128)S(1)} %pad_maximum_fusion), channel_id=1, source_target_pairs={{0,16},{1,25},{2,18},{3,27},{4,20},{5,29},{6,22},{7,31},{8,24},{9,... | collective-permute-start | bytes 98312 | tf_op jit(solution)/shard_map/ppermute | solution.py:119
  12.1 1.2 %collective-permute-start.3 = (f32[32,256]{1,0:T(8,128)S(1)}, f32[32,256]{1,0:T(8,128)S(1)}, u32[]{:S(2)}, u32[]{:S(2)}) collective-permute-start(f32[32,256]{1,0:T(8,128)S(1)} %collective-permute-done.2), channel_id=1, source_target_pairs={{0,1},{1,0},{2,3},{3,2},{4,5},{5,4},{6,7},{7,6},{8,9},{9,8},{10,11... | collective-permute-start | bytes 98312 | tf_op jit(solution)/shard_map/ppermute | solution.py:119
  13.3 3.2 %copy-start = (s32[16]{0:T(128)S(1)}, s32[16]{0:T(128)}, u32[]{:S(2)}) copy-start(s32[16]{0:T(128)} %fine) | copy-start | bytes 196
  13.3 3.2 %copy-start.1 = (s32[32]{0:T(128)S(1)}, s32[32]{0:T(128)}, u32[]{:S(2)}) copy-start(s32[32]{0:T(128)} %mid) | copy-start | bytes 388
  13.3 3.1 %copy-start.2 = (s32[112]{0:T(128)S(1)}, s32[112]{0:T(128)}, u32[]{:S(2)}) copy-start(s32[112]{0:T(128)} %every) | copy-start | bytes 1348
  13.3 5.7 %collective-permute-start.4 = (f32[128,256]{1,0:T(8,128)S(1)}, f32[128,256]{1,0:T(8,128)S(1)}, u32[]{:S(2)}, u32[]{:S(2)}) collective-permute-start(f32[128,256]{1,0:T(8,128)S(1)} %select_dynamic-update-slice_fusion.4), channel_id=1, source_target_pairs={{0,2},{1,5},{2,0},{3,7},{4,6},{5,1},{6,4},{7,3},{8,10},{9,13},{10,... | collective-permute-start | bytes 393224 | tf_op jit(solution)/shard_map/ppermute | solution.py:119
  14.9 5.8 %collective-permute-start.6 = (f32[64,256]{1,0:T(8,128)S(1)}, f32[64,256]{1,0:T(8,128)S(1)}, u32[]{:S(2)}, u32[]{:S(2)}) collective-permute-start(f32[64,256]{1,0:T(8,128)S(1)} %slice_select_fusion), channel_id=1, source_target_pairs={{0,6},{1,7},{2,4},{3,5},{4,2},{5,3},{6,0},{7,1},{8,14},{9,15},{10,... | collective-permute-start | bytes 196616 | tf_op jit(solution)/shard_map/ppermute | solution.py:119
  19.1 1.7 %collective-permute-start.5 = (f32[128,256]{1,0:T(8,128)S(1)}, f32[128,256]{1,0:T(8,128)S(1)}, u32[]{:S(2)}, u32[]{:S(2)}) collective-permute-start(f32[128,256]{1,0:T(8,128)S(1)} %collective-permute-done.4), channel_id=1, source_target_pairs={{0,1},{1,0},{2,3},{3,2},{4,5},{5,4},{6,7},{7,6},{8,9},{9,8},{10,11... | collective-permute-start | bytes 393224 | tf_op jit(solution)/shard_map/ppermute | solution.py:119
  20.7 1.3 %collective-permute-start.7 = (f32[64,256]{1,0:T(8,128)S(1)}, f32[64,256]{1,0:T(8,128)S(1)}, u32[]{:S(2)}, u32[]{:S(2)}) collective-permute-start(f32[64,256]{1,0:T(8,128)S(1)} %settle.3), channel_id=1, source_target_pairs={{0,1},{1,0},{2,3},{3,2},{4,5},{5,4},{6,7},{7,6},{8,9},{9,8},{10,11... | collective-permute-start | bytes 196616 | tf_op jit(solution)/shard_map/ppermute | solution.py:119

commit v2 on v1

--- a/solution.py
+++ b/solution.py
@@ -133,22 +133,28 @@
             parts = [block, fetch(block, stride, stride)]
         elif last:
             half = block.shape[0] // 2
-            one = fetch(block, stride, 2 * stride)
+            one = fetch(block, stride, 3 * stride)
             two = jnp.where(odd, block[half:], block[:half])
-            two = settle(fetch(two, 3 * stride, 3 * stride))
+            two = settle(fetch(two, 2 * stride, 2 * stride))
             parts = [block] + both(one, fetch(one, 1, 1)) + both(two, fetch(two, 1, 1))
         else:
             one = fetch(block, 2 * stride, 3 * stride)
             near = settle(fetch(block, stride, stride))
-            parts = [block, near] + both(one, fetch(one, 1, 1))
+            second, third = both(one, fetch(one, 1, 1))
+            parts = [block, second, near, third]
         block = jnp.concatenate(parts, axis=0)
     return block, planned
 
 
 def slot_of(device, me, devices):
     slot, held = device % 2, 2
-    for stride, radix in rounds_of(devices):
-        slot = slot + (device ^ me) // stride % radix * held
+    rounds = rounds_of(devices)
+    for stride, radix in rounds:
+        digit = (device ^ me) // stride % radix
+        if radix == 4:
+            last = stride == rounds[-1][0]
+            digit = digit ^ (digit // 2) if last else digit // 2 + digit % 2 * 2
+        slot = slot + digit * held
         held *= radix
     return slot
 

time: 29.2 us -> 27.4 us (0.938); the launches traced: 29.3 us -> 27 us
  waiting for transfers between devices: 8.84 us -> 5.95 us
  starting transfers between devices: 9.22 us -> 9.89 us
    ppermute x8, waiting for transfers between devices: 8.84 us -> 5.95 us  [fetch(): return lax.ppermute(value, 'stars', pairs)]
    ppermute x8, starting transfers between devices: 9.22 us -> 9.89 us  [fetch(): return lax.ppermute(value, 'stars', pairs)]
where the time goes in v2:
time: 27.4 us; the launch traced here: 27 us
  Pallas kernels  10.2 us (37%)
  starting transfers between devices  9.89 us (36%)
  waiting for transfers between devices  5.95 us (22%)
  between operations  0.76 us (3%)
    ppermute x8, starting transfers between devices, fetch(): return lax.ppermute(value, 'stars', pairs)  9.89 us
    pallas_call x1, Pallas kernels, body(): pl.pallas_call(functools.partial(main_kernel, devices, own_count, sizes),...  7.16 us
    ppermute x8, waiting for transfers between devices, fetch(): return lax.ppermute(value, 'stars', pairs)  5.95 us
    pallas_call x1, Pallas kernels, plan(): pl.pallas_call(functools.partial(plan_kernel, own_count), out_shape=jax.S...  1.67 us
    pallas_call x1, Pallas kernels, body(): pl.pallas_call(pack_kernel, out_shape=jax.ShapeDtypeStruct((16, own_count...  1.42 us
  transfers between devices with their start and end apart: 8, of which 6 were waited for; matrix products, arithmetic and copies ran while one was open for 0% of the time, Pallas kernels for 6%

profile of v2, /device:TPU:0, one launch (start us, length us, event | category | flops | bytes accessed | tf_op | source)
XLA Modules:
  0.0 27.0 jit_solution(18146999623280376973)
XLA Ops:
  0.6 1.4 %pack.1 = f32[16,256]{1,0:T(8,128)} custom-call(f32[3,256]{1,0:T(4,128)} %place.1, f32[3,256]{1,0:T(4,128)} %motion.1, f32[3,256]{1,0:T(4,128)} %pull.1, f32[3,256]{1,0:T(4,128)} %change.1, f32[2,128]{1,0:T(2,128)} %bitcast.2, s32[2,128]{1,0:T(2,128)} %bitcast.3), custom_call_target="tpu_custom_call" | custom-call | tf_op jit(solution)/shard_map/pack/pallas_call | solution.py:441
  2.1 0.0 copy-start.3
  2.1 0.5 %collective-permute-start = (f32[16,256]{1,0:T(8,128)}, f32[16,256]{1,0:T(8,128)S(1)}, u32[]{:S(2)}, u32[]{:S(2)}) collective-permute-start(f32[16,256]{1,0:T(8,128)} %pack.1), channel_id=1, source_target_pairs={{0,1},{1,0},{2,3},{3,2},{4,5},{5,4},{6,7},{7,6},{8,9},{9,8},{10,11... | collective-permute-start | bytes 49160 | tf_op jit(solution)/shard_map/ppermute | solution.py:119
  2.6 1.0 %collective-permute-done = f32[16,256]{1,0:T(8,128)S(1)} collective-permute-done((f32[16,256]{1,0:T(8,128)}, f32[16,256]{1,0:T(8,128)S(1)}, u32[]{:S(2)}, u32[]{:S(2)}) %collective-permute-start) | collective-permute-done | bytes 16416 | tf_op jit(solution)/shard_map/ppermute | solution.py:119
  3.6 0.0 copy-done.3
  3.7 4.0 %collective-permute-start.1 = (f32[32,256]{1,0:T(8,128)S(1)}, f32[32,256]{1,0:T(8,128)S(1)}, u32[]{:S(2)}, u32[]{:S(2)}) collective-permute-start(f32[32,256]{1,0:T(8,128)S(1)} %pad_maximum_fusion), channel_id=1, source_target_pairs={{0,16},{1,25},{2,18},{3,27},{4,20},{5,29},{6,22},{7,31},{8,24},{9,... | collective-permute-start | bytes 98312 | tf_op jit(solution)/shard_map/ppermute | solution.py:119
  7.7 1.6 %collective-permute-start.3 = (f32[32,256]{1,0:T(8,128)S(1)}, f32[32,256]{1,0:T(8,128)S(1)}, u32[]{:S(2)}, u32[]{:S(2)}) collective-permute-start(f32[32,256]{1,0:T(8,128)S(1)} %pad_maximum_fusion), channel_id=1, source_target_pairs={{0,8},{1,9},{2,10},{3,11},{4,12},{5,13},{6,14},{7,15},{8,0},{9,1},... | collective-permute-start | bytes 98312 | tf_op jit(solution)/shard_map/ppermute | solution.py:119
  9.3 0.3 %collective-permute-done.1 = f32[32,256]{1,0:T(8,128)S(1)} collective-permute-done((f32[32,256]{1,0:T(8,128)S(1)}, f32[32,256]{1,0:T(8,128)S(1)}, u32[]{:S(2)}, u32[]{:S(2)}) %collective-permute-start.1) | collective-permute-done | bytes 32800 | tf_op jit(solution)/shard_map/ppermute | solution.py:119
  9.6 0.3 %collective-permute-start.2 = (f32[32,256]{1,0:T(8,128)S(1)}, f32[32,256]{1,0:T(8,128)S(1)}, u32[]{:S(2)}, u32[]{:S(2)}) collective-permute-start(f32[32,256]{1,0:T(8,128)S(1)} %collective-permute-done.1), channel_id=1, source_target_pairs={{0,1},{1,0},{2,3},{3,2},{4,5},{5,4},{6,7},{7,6},{8,9},{9,8},{10,11... | collective-permute-start | bytes 98312 | tf_op jit(solution)/shard_map/ppermute | solution.py:119
  9.9 2.0 %collective-permute-done.3.source = f32[32,256]{1,0:T(8,128)S(1)} collective-permute-done((f32[32,256]{1,0:T(8,128)S(1)}, f32[32,256]{1,0:T(8,128)S(1)}, u32[]{:S(2)}, u32[]{:S(2)}) %collective-permute-start.3) | collective-permute-done | bytes 32800 | tf_op jit(solution)/shard_map/ppermute | solution.py:119
  11.9 0.0 collective-permute-done.2
  11.9 0.0 copy-start
  11.9 0.0 copy-start.1
  11.9 0.0 copy-start.2
  11.9 1.6 %collective-permute-start.4 = (f32[128,256]{1,0:T(8,128)S(1)}, f32[128,256]{1,0:T(8,128)S(1)}, u32[]{:S(2)}, u32[]{:S(2)}) collective-permute-start(f32[128,256]{1,0:T(8,128)S(1)} %select_dynamic-update-slice_fusion.4), channel_id=1, source_target_pairs={{0,2},{1,7},{2,0},{3,5},{4,6},{5,3},{6,4},{7,1},{8,10},{9,15},{10,... | collective-permute-start | bytes 393224 | tf_op jit(solution)/shard_map/ppermute | solution.py:119
  13.5 1.6 %collective-permute-start.6 = (f32[64,256]{1,0:T(8,128)S(1)}, f32[64,256]{1,0:T(8,128)S(1)}, u32[]{:S(2)}, u32[]{:S(2)}) collective-permute-start(f32[64,256]{1,0:T(8,128)S(1)} %slice_select_fusion), channel_id=1, source_target_pairs={{0,4},{1,5},{2,6},{3,7},{4,0},{5,1},{6,2},{7,3},{8,12},{9,13},{10,... | collective-permute-start | bytes 196616 | tf_op jit(solution)/shard_map/ppermute | solution.py:119
  15.1 0.0 copy-done
  15.1 0.0 copy-done.1
  15.1 0.0 copy-done.2
  15.1 1.7 %plan.1.listed = s32[152]{0:T(256)S(1)} custom-call(s32[16]{0:T(128)S(1)} %copy-done, s32[32]{0:T(128)S(1)} %copy-done.1, s32[112]{0:T(128)S(1)} %copy-done.2), custom_call_target="tpu_custom_call" | custom-call | tf_op jit(solution)/shard_map/plan/pallas_call | solution.py:451
  16.8 1.6 %collective-permute-done.4 = f32[128,256]{1,0:T(8,128)S(1)} collective-permute-done((f32[128,256]{1,0:T(8,128)S(1)}, f32[128,256]{1,0:T(8,128)S(1)}, u32[]{:S(2)}, u32[]{:S(2)}) %collective-permute-start.4) | collective-permute-done | bytes 131104 | tf_op jit(solution)/shard_map/ppermute | solution.py:119
  18.4 0.0 collective-permute-start.5
  18.4 0.2 collective-permute-done.6.source
  18.5 0.4 %collective-permute-start.7 = (f32[64,256]{1,0:T(8,128)S(1)}, f32[64,256]{1,0:T(8,128)S(1)}, u32[]{:S(2)}, u32[]{:S(2)}) collective-permute-start(f32[64,256]{1,0:T(8,128)S(1)} %settle.3), channel_id=1, source_target_pairs={{0,1},{1,0},{2,3},{3,2},{4,5},{5,4},{6,7},{7,6},{8,9},{9,8},{10,11... | collective-permute-start | bytes 196616 | tf_op jit(solution)/shard_map/ppermute | solution.py:119
  18.9 0.8 %collective-permute-done.5 = f32[128,256]{1,0:T(8,128)S(1)} collective-permute-done((f32[128,256]{1,0:T(8,128)S(1)}, f32[128,256]{1,0:T(8,128)S(1)}, u32[]{:S(2)}, u32[]{:S(2)}) %collective-permute-start.5) | collective-permute-done | bytes 131104 | tf_op jit(solution)/shard_map/ppermute | solution.py:119
  19.8 0.0 collective-permute-done.7
  19.8 7.2 %steps.1 = (f32[3,256]{1,0:T(4,128)}, f32[3,256]{1,0:T(4,128)}, f32[3,256]{1,0:T(4,128)}, f32[3,256]{1,0:T(4,128)}) custom-call(s32[152]{0:T(256)S(1)} %plan.1.listed, f32[512,256]{1,0:T(8,128)S(1)} %select_dynamic-update-slice_fusion.2.field), custom_call_target="tpu_custom_call" | custom-call | tf_op jit(solution)/shard_map/steps/pallas_call | solution.py:463
  (14 shorter events, 0.1 us)
Async XLA Ops:
  2.1 1.6 %copy-start.3 = (f32[16,256]{1,0:T(8,128)S(1)}, f32[16,256]{1,0:T(8,128)}, u32[]{:S(2)}) copy-start(f32[16,256]{1,0:T(8,128)} %pack.1) | copy-start | bytes 49156
  2.1 1.6 %collective-permute-start = (f32[16,256]{1,0:T(8,128)}, f32[16,256]{1,0:T(8,128)S(1)}, u32[]{:S(2)}, u32[]{:S(2)}) collective-permute-start(f32[16,256]{1,0:T(8,128)} %pack.1), channel_id=1, source_target_pairs={{0,1},{1,0},{2,3},{3,2},{4,5},{5,4},{6,7},{7,6},{8,9},{9,8},{10,11... | collective-permute-start | bytes 49160 | tf_op jit(solution)/shard_map/ppermute | solution.py:119
  3.7 5.9 %collective-permute-start.1 = (f32[32,256]{1,0:T(8,128)S(1)}, f32[32,256]{1,0:T(8,128)S(1)}, u32[]{:S(2)}, u32[]{:S(2)}) collective-permute-start(f32[32,256]{1,0:T(8,128)S(1)} %pad_maximum_fusion), channel_id=1, source_target_pairs={{0,16},{1,25},{2,18},{3,27},{4,20},{5,29},{6,22},{7,31},{8,24},{9,... | collective-permute-start | bytes 98312 | tf_op jit(solution)/shard_map/ppermute | solution.py:119
  7.7 4.2 %collective-permute-start.3 = (f32[32,256]{1,0:T(8,128)S(1)}, f32[32,256]{1,0:T(8,128)S(1)}, u32[]{:S(2)}, u32[]{:S(2)}) collective-permute-start(f32[32,256]{1,0:T(8,128)S(1)} %pad_maximum_fusion), channel_id=1, source_target_pairs={{0,8},{1,9},{2,10},{3,11},{4,12},{5,13},{6,14},{7,15},{8,0},{9,1},... | collective-permute-start | bytes 98312 | tf_op jit(solution)/shard_map/ppermute | solution.py:119
  9.6 2.3 %collective-permute-start.2 = (f32[32,256]{1,0:T(8,128)S(1)}, f32[32,256]{1,0:T(8,128)S(1)}, u32[]{:S(2)}, u32[]{:S(2)}) collective-permute-start(f32[32,256]{1,0:T(8,128)S(1)} %collective-permute-done.1), channel_id=1, source_target_pairs={{0,1},{1,0},{2,3},{3,2},{4,5},{5,4},{6,7},{7,6},{8,9},{9,8},{10,11... | collective-permute-start | bytes 98312 | tf_op jit(solution)/shard_map/ppermute | solution.py:119
  11.9 3.2 %copy-start = (s32[16]{0:T(128)S(1)}, s32[16]{0:T(128)}, u32[]{:S(2)}) copy-start(s32[16]{0:T(128)} %fine) | copy-start | bytes 196
  11.9 3.2 %copy-start.1 = (s32[32]{0:T(128)S(1)}, s32[32]{0:T(128)}, u32[]{:S(2)}) copy-start(s32[32]{0:T(128)} %mid) | copy-start | bytes 388
  11.9 3.2 %copy-start.2 = (s32[112]{0:T(128)S(1)}, s32[112]{0:T(128)}, u32[]{:S(2)}) copy-start(s32[112]{0:T(128)} %every) | copy-start | bytes 1348
  11.9 6.4 %collective-permute-start.4 = (f32[128,256]{1,0:T(8,128)S(1)}, f32[128,256]{1,0:T(8,128)S(1)}, u32[]{:S(2)}, u32[]{:S(2)}) collective-permute-start(f32[128,256]{1,0:T(8,128)S(1)} %select_dynamic-update-slice_fusion.4), channel_id=1, source_target_pairs={{0,2},{1,7},{2,0},{3,5},{4,6},{5,3},{6,4},{7,1},{8,10},{9,15},{10,... | collective-permute-start | bytes 393224 | tf_op jit(solution)/shard_map/ppermute | solution.py:119
  13.5 5.0 %collective-permute-start.6 = (f32[64,256]{1,0:T(8,128)S(1)}, f32[64,256]{1,0:T(8,128)S(1)}, u32[]{:S(2)}, u32[]{:S(2)}) collective-permute-start(f32[64,256]{1,0:T(8,128)S(1)} %slice_select_fusion), channel_id=1, source_target_pairs={{0,4},{1,5},{2,6},{3,7},{4,0},{5,1},{6,2},{7,3},{8,12},{9,13},{10,... | collective-permute-start | bytes 196616 | tf_op jit(solution)/shard_map/ppermute | solution.py:119
  18.4 1.3 %collective-permute-start.5 = (f32[128,256]{1,0:T(8,128)S(1)}, f32[128,256]{1,0:T(8,128)S(1)}, u32[]{:S(2)}, u32[]{:S(2)}) collective-permute-start(f32[128,256]{1,0:T(8,128)S(1)} %collective-permute-done.4), channel_id=1, source_target_pairs={{0,1},{1,0},{2,3},{3,2},{4,5},{5,4},{6,7},{7,6},{8,9},{9,8},{10,11... | collective-permute-start | bytes 393224 | tf_op jit(solution)/shard_map/ppermute | solution.py:119
  18.5 1.3 %collective-permute-start.7 = (f32[64,256]{1,0:T(8,128)S(1)}, f32[64,256]{1,0:T(8,128)S(1)}, u32[]{:S(2)}, u32[]{:S(2)}) collective-permute-start(f32[64,256]{1,0:T(8,128)S(1)} %settle.3), channel_id=1, source_target_pairs={{0,1},{1,0},{2,3},{3,2},{4,5},{5,4},{6,7},{7,6},{8,9},{9,8},{10,11... | collective-permute-start | bytes 196616 | tf_op jit(solution)/shard_map/ppermute | solution.py:119

commit v3 on v2

--- a/solution.py
+++ b/solution.py
@@ -49,8 +49,9 @@
         out[11:12, at] = level_at[row, :].astype(jnp.float32)
 
 
-def plan_kernel(own, fine, mid, every, listed):
-    first = lax.axis_index("stars") * own
+def plan_kernel(devices, own, fine, mid, every, listed):
+    me = lax.axis_index("stars")
+    first = me * own
     count_fine, count_mid, count_all = fine.shape[0], mid.shape[0], every.shape[0]
     order = 2 + count_all
 
@@ -71,6 +72,15 @@
 
     keep(fine, order)
     keep(every, 2)
+
+    def locate(index, carry):
+        star = listed[order + index]
+        device = star >> (own.bit_length() - 1)
+        listed[order + count_mid + index] = slot_of(device, me, devices) * 16
+        listed[order + 2 * count_mid + index] = star & lanes
+        return carry
+
+    lax.fori_loop(0, count_mid, locate, 0, unroll=8)
 
     def below(bound):
         found = jnp.int32(0)
@@ -147,15 +157,15 @@
 
 
 def slot_of(device, me, devices):
-    slot, held = device % 2, 2
+    slot, shift = device & 1, 1
     rounds = rounds_of(devices)
     for stride, radix in rounds:
-        digit = (device ^ me) // stride % radix
+        digit = ((device ^ me) >> (stride.bit_length() - 1)) & (radix - 1)
         if radix == 4:
             last = stride == rounds[-1][0]
-            digit = digit ^ (digit // 2) if last else digit // 2 + digit % 2 * 2
-        slot = slot + digit * held
-        held *= radix
+            digit = digit ^ (digit >> 1) if last else (digit >> 1) | ((digit & 1) << 1)
+        slot = slot | (digit << shift)
+        shift += radix.bit_length() - 1
     return slot
 
 
@@ -178,7 +188,7 @@
     devices,
     own_count,
     sizes,
-    listed,
+    listed_from,
     field,
     out_place,
     out_motion,
@@ -193,6 +203,8 @@
     mid_state,
     mid_names,
     result,
+    listed,
+    arrived,
 ):
     count_fine, count_mid, count_all = sizes
     blocks, blocks_fine = count_mid // 8, count_fine // 8
@@ -219,6 +231,9 @@
     halves = [slice(0, lanes), slice(lanes, 2 * lanes)]
     me = lax.axis_index("stars")
     first = me * own_count
+
+    copy = pltpu.make_async_copy(listed_from, listed, arrived)
+    copy.start()
 
     def look_ahead(index):
         for half in range(2):
@@ -240,6 +255,7 @@
         for inner in range(together):
             look_ahead(index * together + inner)
 
+    copy.wait()
     low, count = listed[0], listed[1]
 
     mine = pl.multiple_of(slot_of(me, me, devices) * 16, 16)
@@ -252,13 +268,14 @@
     def fetch(block):
         name = jnp.zeros((8, lanes), jnp.int32)
         for row in range(8):
-            star = listed[2 + count_all + block * 8 + row]
-            base = pl.multiple_of(slot_of(star // own_count, me, devices) * 16, 16)
-            side = pl.multiple_of(star % own_count // lanes * lanes, lanes)
+            at = 2 + count_all + block * 8 + row
+            star = listed[at]
+            base = pl.multiple_of(listed[at + count_mid], 16)
+            side = pl.multiple_of(listed[at + 2 * count_mid], lanes)
             slab[16 * row : 16 * row + 16, :] = field[pl.ds(base, 16), pl.ds(side, lanes)]
             name = jnp.where(sub == row, star, name)
         names[rows8(block), :] = name
-        hit = (name % lanes) == lane
+        hit = (name & (lanes - 1)) == lane
         for part in range(4):
             for component in range(3):
                 value = slab[pl.ds(4 * part + component, 8, stride=16), :]
@@ -434,6 +451,7 @@
 
 def body(devices, place, motion, pull, change, masses, star_level, fine, mid, every):
     own_count = place.shape[1]
+    assert own_count == 2 * lanes
     sizes = (fine.shape[0], mid.shape[0], every.shape[0])
     groups = -(-sizes[1] // lanes)
     held = [pltpu.VMEM((3, own_count), jnp.float32)] * 4
@@ -447,10 +465,12 @@
         name="pack",
     )(place, motion, pull, change, masses.reshape(2, lanes), star_level.reshape(2, lanes))
 
+    listed_shape = (2 + sizes[2] + 3 * sizes[1],)
+
     def plan(lists):
         return pl.pallas_call(
-            functools.partial(plan_kernel, own_count),
-            out_shape=jax.ShapeDtypeStruct((2 + sizes[2] + sizes[1] + 6,), jnp.int32),
+            functools.partial(plan_kernel, devices, own_count),
+            out_shape=jax.ShapeDtypeStruct(listed_shape, jnp.int32),
             in_specs=[smem] * 3,
             out_specs=smem,
             compiler_params=pltpu.CompilerParams(vmem_limit_bytes=1024 * 1024),
@@ -463,7 +483,7 @@
     return pl.pallas_call(
         functools.partial(main_kernel, devices, own_count, sizes),
         out_shape=(result,) * 4,
-        in_specs=[smem, vmem],
+        in_specs=[pl.BlockSpec(memory_space=pl.ANY), vmem],
         out_specs=(vmem,) * 4,
         scratch_shapes=[
             pltpu.VMEM((4, devices * 2, 8, lanes), jnp.float32),
@@ -475,6 +495,8 @@
             pltpu.VMEM((groups, 16, lanes), jnp.float32),
             pltpu.VMEM((groups, 8, lanes), jnp.int32),
             pltpu.VMEM((4, 2, 3, 8, lanes), jnp.float32),
+            pltpu.SMEM(listed_shape, jnp.int32),
+            pltpu.SemaphoreType.DMA,
         ],
         compiler_params=pltpu.CompilerParams(vmem_limit_bytes=room),
         name="steps",

time: 27.4 us -> 25.8 us (0.942)
  Pallas kernels: 10.2 us -> 9.15 us
  waiting for transfers between devices: 5.95 us -> 5.65 us
    pallas_call x1, Pallas kernels: 7.16 us -> 5.75 us  [body(): pl.pallas_call(functools.partial(main_kernel, devices, own_count, sizes),...]
    pallas_call x1, Pallas kernels: 1.67 us -> 1.97 us  [plan(): pl.pallas_call(functools.partial(plan_kernel, devices, own_count), out_sh...]
    ppermute x8, waiting for transfers between devices: 5.95 us -> 5.65 us  [fetch(): return lax.ppermute(value, 'stars', pairs)]
  transfers between devices with their start and end apart: 8 -> 8, of which waited for: 6 -> 6; matrix products, arithmetic and copies ran while one was open for 0% -> 0% of each run, Pallas kernels for 6% -> 8%
where the time goes in v3:
time: 25.8 us; the launch traced here: 25.6 us
  starting transfers between devices  9.89 us (38%)
  Pallas kernels  9.15 us (35%)
  waiting for transfers between devices  5.65 us (22%)
  between operations  0.76 us (3%)
    ppermute x8, starting transfers between devices, fetch(): return lax.ppermute(value, 'stars', pairs)  9.89 us
    pallas_call x1, Pallas kernels, body(): pl.pallas_call(functools.partial(main_kernel, devices, own_count, sizes),...  5.75 us
    ppermute x8, waiting for transfers between devices, fetch(): return lax.ppermute(value, 'stars', pairs)  5.65 us
    pallas_call x1, Pallas kernels, plan(): pl.pallas_call(functools.partial(plan_kernel, devices, own_count), out_sh...  1.97 us
    pallas_call x1, Pallas kernels, body(): pl.pallas_call(pack_kernel, out_shape=jax.ShapeDtypeStruct((16, own_count...  1.42 us
  transfers between devices with their start and end apart: 8, of which 6 were waited for; matrix products, arithmetic and copies ran while one was open for 0% of the time, Pallas kernels for 8%

profile of v3, /device:TPU:0, one launch (start us, length us, event | category | flops | bytes accessed | tf_op | source)
XLA Modules:
  0.0 25.6 jit_solution(5578207213945909305)
XLA Ops:
  0.6 1.4 %pack.1 = f32[16,256]{1,0:T(8,128)} custom-call(f32[3,256]{1,0:T(4,128)} %place.1, f32[3,256]{1,0:T(4,128)} %motion.1, f32[3,256]{1,0:T(4,128)} %pull.1, f32[3,256]{1,0:T(4,128)} %change.1, f32[2,128]{1,0:T(2,128)} %bitcast.2, s32[2,128]{1,0:T(2,128)} %bitcast.3), custom_call_target="tpu_custom_call" | custom-call | tf_op jit(solution)/shard_map/pack/pallas_call | solution.py:459
  2.1 0.0 copy-start.3
  2.1 0.5 %collective-permute-start = (f32[16,256]{1,0:T(8,128)}, f32[16,256]{1,0:T(8,128)S(1)}, u32[]{:S(2)}, u32[]{:S(2)}) collective-permute-start(f32[16,256]{1,0:T(8,128)} %pack.1), channel_id=1, source_target_pairs={{0,1},{1,0},{2,3},{3,2},{4,5},{5,4},{6,7},{7,6},{8,9},{9,8},{10,11... | collective-permute-start | bytes 49160 | tf_op jit(solution)/shard_map/ppermute | solution.py:129
  2.6 1.0 %collective-permute-done = f32[16,256]{1,0:T(8,128)S(1)} collective-permute-done((f32[16,256]{1,0:T(8,128)}, f32[16,256]{1,0:T(8,128)S(1)}, u32[]{:S(2)}, u32[]{:S(2)}) %collective-permute-start) | collective-permute-done | bytes 16416 | tf_op jit(solution)/shard_map/ppermute | solution.py:129
  3.6 0.0 copy-done.3
  3.7 4.0 %collective-permute-start.1 = (f32[32,256]{1,0:T(8,128)S(1)}, f32[32,256]{1,0:T(8,128)S(1)}, u32[]{:S(2)}, u32[]{:S(2)}) collective-permute-start(f32[32,256]{1,0:T(8,128)S(1)} %pad_maximum_fusion), channel_id=1, source_target_pairs={{0,16},{1,25},{2,18},{3,27},{4,20},{5,29},{6,22},{7,31},{8,24},{9,... | collective-permute-start | bytes 98312 | tf_op jit(solution)/shard_map/ppermute | solution.py:129
  7.7 1.6 %collective-permute-start.3 = (f32[32,256]{1,0:T(8,128)S(1)}, f32[32,256]{1,0:T(8,128)S(1)}, u32[]{:S(2)}, u32[]{:S(2)}) collective-permute-start(f32[32,256]{1,0:T(8,128)S(1)} %pad_maximum_fusion), channel_id=1, source_target_pairs={{0,8},{1,9},{2,10},{3,11},{4,12},{5,13},{6,14},{7,15},{8,0},{9,1},... | collective-permute-start | bytes 98312 | tf_op jit(solution)/shard_map/ppermute | solution.py:129
  9.3 0.3 %collective-permute-done.1 = f32[32,256]{1,0:T(8,128)S(1)} collective-permute-done((f32[32,256]{1,0:T(8,128)S(1)}, f32[32,256]{1,0:T(8,128)S(1)}, u32[]{:S(2)}, u32[]{:S(2)}) %collective-permute-start.1) | collective-permute-done | bytes 32800 | tf_op jit(solution)/shard_map/ppermute | solution.py:129
  9.6 0.3 %collective-permute-start.2 = (f32[32,256]{1,0:T(8,128)S(1)}, f32[32,256]{1,0:T(8,128)S(1)}, u32[]{:S(2)}, u32[]{:S(2)}) collective-permute-start(f32[32,256]{1,0:T(8,128)S(1)} %collective-permute-done.1), channel_id=1, source_target_pairs={{0,1},{1,0},{2,3},{3,2},{4,5},{5,4},{6,7},{7,6},{8,9},{9,8},{10,11... | collective-permute-start | bytes 98312 | tf_op jit(solution)/shard_map/ppermute | solution.py:129
  9.9 2.0 %collective-permute-done.3.source = f32[32,256]{1,0:T(8,128)S(1)} collective-permute-done((f32[32,256]{1,0:T(8,128)S(1)}, f32[32,256]{1,0:T(8,128)S(1)}, u32[]{:S(2)}, u32[]{:S(2)}) %collective-permute-start.3) | collective-permute-done | bytes 32800 | tf_op jit(solution)/shard_map/ppermute | solution.py:129
  11.9 0.0 collective-permute-done.2
  11.9 0.0 copy-start
  11.9 0.0 copy-start.1
  11.9 0.0 copy-start.2
  11.9 1.6 %collective-permute-start.4 = (f32[128,256]{1,0:T(8,128)S(1)}, f32[128,256]{1,0:T(8,128)S(1)}, u32[]{:S(2)}, u32[]{:S(2)}) collective-permute-start(f32[128,256]{1,0:T(8,128)S(1)} %select_dynamic-update-slice_fusion.4), channel_id=1, source_target_pairs={{0,2},{1,7},{2,0},{3,5},{4,6},{5,3},{6,4},{7,1},{8,10},{9,15},{10,... | collective-permute-start | bytes 393224 | tf_op jit(solution)/shard_map/ppermute | solution.py:129
  13.5 1.6 %collective-permute-start.6 = (f32[64,256]{1,0:T(8,128)S(1)}, f32[64,256]{1,0:T(8,128)S(1)}, u32[]{:S(2)}, u32[]{:S(2)}) collective-permute-start(f32[64,256]{1,0:T(8,128)S(1)} %slice_select_fusion), channel_id=1, source_target_pairs={{0,4},{1,5},{2,6},{3,7},{4,0},{5,1},{6,2},{7,3},{8,12},{9,13},{10,... | collective-permute-start | bytes 196616 | tf_op jit(solution)/shard_map/ppermute | solution.py:129
  15.1 0.0 copy-done
  15.1 0.0 copy-done.1
  15.1 0.0 copy-done.2
  15.1 2.0 %plan.1.listed_from = s32[210]{0:T(256)S(1)} custom-call(s32[16]{0:T(128)S(1)} %copy-done, s32[32]{0:T(128)S(1)} %copy-done.1, s32[112]{0:T(128)S(1)} %copy-done.2), custom_call_target="tpu_custom_call" | custom-call | tf_op jit(solution)/shard_map/plan/pallas_call | solution.py:471
  17.1 1.3 %collective-permute-done.4 = f32[128,256]{1,0:T(8,128)S(1)} collective-permute-done((f32[128,256]{1,0:T(8,128)S(1)}, f32[128,256]{1,0:T(8,128)S(1)}, u32[]{:S(2)}, u32[]{:S(2)}) %collective-permute-start.4) | collective-permute-done | bytes 131104 | tf_op jit(solution)/shard_map/ppermute | solution.py:129
  18.4 0.0 collective-permute-start.5
  18.4 0.2 collective-permute-done.6.source
  18.5 0.4 %collective-permute-start.7 = (f32[64,256]{1,0:T(8,128)S(1)}, f32[64,256]{1,0:T(8,128)S(1)}, u32[]{:S(2)}, u32[]{:S(2)}) collective-permute-start(f32[64,256]{1,0:T(8,128)S(1)} %settle.3), channel_id=1, source_target_pairs={{0,1},{1,0},{2,3},{3,2},{4,5},{5,4},{6,7},{7,6},{8,9},{9,8},{10,11... | collective-permute-start | bytes 196616 | tf_op jit(solution)/shard_map/ppermute | solution.py:129
  18.9 0.8 %collective-permute-done.5 = f32[128,256]{1,0:T(8,128)S(1)} collective-permute-done((f32[128,256]{1,0:T(8,128)S(1)}, f32[128,256]{1,0:T(8,128)S(1)}, u32[]{:S(2)}, u32[]{:S(2)}) %collective-permute-start.5) | collective-permute-done | bytes 131104 | tf_op jit(solution)/shard_map/ppermute | solution.py:129
  19.8 0.0 collective-permute-done.7
  19.8 5.8 %steps.1 = (f32[3,256]{1,0:T(4,128)}, f32[3,256]{1,0:T(4,128)}, f32[3,256]{1,0:T(4,128)}, f32[3,256]{1,0:T(4,128)}) custom-call(s32[210]{0:T(256)S(1)} %plan.1.listed_from, f32[512,256]{1,0:T(8,128)S(1)} %select_dynamic-update-slice_fusion.2.field), custom_call_target="tpu_custom_call" | custom-call | tf_op jit(solution)/shard_map/steps/pallas_call | solution.py:483
  (14 shorter events, 0.1 us)
Async XLA Ops:
  2.1 1.6 %copy-start.3 = (f32[16,256]{1,0:T(8,128)S(1)}, f32[16,256]{1,0:T(8,128)}, u32[]{:S(2)}) copy-start(f32[16,256]{1,0:T(8,128)} %pack.1) | copy-start | bytes 49156
  2.1 1.6 %collective-permute-start = (f32[16,256]{1,0:T(8,128)}, f32[16,256]{1,0:T(8,128)S(1)}, u32[]{:S(2)}, u32[]{:S(2)}) collective-permute-start(f32[16,256]{1,0:T(8,128)} %pack.1), channel_id=1, source_target_pairs={{0,1},{1,0},{2,3},{3,2},{4,5},{5,4},{6,7},{7,6},{8,9},{9,8},{10,11... | collective-permute-start | bytes 49160 | tf_op jit(solution)/shard_map/ppermute | solution.py:129
  3.7 5.9 %collective-permute-start.1 = (f32[32,256]{1,0:T(8,128)S(1)}, f32[32,256]{1,0:T(8,128)S(1)}, u32[]{:S(2)}, u32[]{:S(2)}) collective-permute-start(f32[32,256]{1,0:T(8,128)S(1)} %pad_maximum_fusion), channel_id=1, source_target_pairs={{0,16},{1,25},{2,18},{3,27},{4,20},{5,29},{6,22},{7,31},{8,24},{9,... | collective-permute-start | bytes 98312 | tf_op jit(solution)/shard_map/ppermute | solution.py:129
  7.7 4.2 %collective-permute-start.3 = (f32[32,256]{1,0:T(8,128)S(1)}, f32[32,256]{1,0:T(8,128)S(1)}, u32[]{:S(2)}, u32[]{:S(2)}) collective-permute-start(f32[32,256]{1,0:T(8,128)S(1)} %pad_maximum_fusion), channel_id=1, source_target_pairs={{0,8},{1,9},{2,10},{3,11},{4,12},{5,13},{6,14},{7,15},{8,0},{9,1},... | collective-permute-start | bytes 98312 | tf_op jit(solution)/shard_map/ppermute | solution.py:129
  9.6 2.3 %collective-permute-start.2 = (f32[32,256]{1,0:T(8,128)S(1)}, f32[32,256]{1,0:T(8,128)S(1)}, u32[]{:S(2)}, u32[]{:S(2)}) collective-permute-start(f32[32,256]{1,0:T(8,128)S(1)} %collective-permute-done.1), channel_id=1, source_target_pairs={{0,1},{1,0},{2,3},{3,2},{4,5},{5,4},{6,7},{7,6},{8,9},{9,8},{10,11... | collective-permute-start | bytes 98312 | tf_op jit(solution)/shard_map/ppermute | solution.py:129
  11.9 3.2 %copy-start = (s32[16]{0:T(128)S(1)}, s32[16]{0:T(128)}, u32[]{:S(2)}) copy-start(s32[16]{0:T(128)} %fine) | copy-start | bytes 196
  11.9 3.2 %copy-start.1 = (s32[32]{0:T(128)S(1)}, s32[32]{0:T(128)}, u32[]{:S(2)}) copy-start(s32[32]{0:T(128)} %mid) | copy-start | bytes 388
  11.9 3.2 %copy-start.2 = (s32[112]{0:T(128)S(1)}, s32[112]{0:T(128)}, u32[]{:S(2)}) copy-start(s32[112]{0:T(128)} %every) | copy-start | bytes 1348
  11.9 6.4 %collective-permute-start.4 = (f32[128,256]{1,0:T(8,128)S(1)}, f32[128,256]{1,0:T(8,128)S(1)}, u32[]{:S(2)}, u32[]{:S(2)}) collective-permute-start(f32[128,256]{1,0:T(8,128)S(1)} %select_dynamic-update-slice_fusion.4), channel_id=1, source_target_pairs={{0,2},{1,7},{2,0},{3,5},{4,6},{5,3},{6,4},{7,1},{8,10},{9,15},{10,... | collective-permute-start | bytes 393224 | tf_op jit(solution)/shard_map/ppermute | solution.py:129
  13.5 5.0 %collective-permute-start.6 = (f32[64,256]{1,0:T(8,128)S(1)}, f32[64,256]{1,0:T(8,128)S(1)}, u32[]{:S(2)}, u32[]{:S(2)}) collective-permute-start(f32[64,256]{1,0:T(8,128)S(1)} %slice_select_fusion), channel_id=1, source_target_pairs={{0,4},{1,5},{2,6},{3,7},{4,0},{5,1},{6,2},{7,3},{8,12},{9,13},{10,... | collective-permute-start | bytes 196616 | tf_op jit(solution)/shard_map/ppermute | solution.py:129
  18.4 1.3 %collective-permute-start.5 = (f32[128,256]{1,0:T(8,128)S(1)}, f32[128,256]{1,0:T(8,128)S(1)}, u32[]{:S(2)}, u32[]{:S(2)}) collective-permute-start(f32[128,256]{1,0:T(8,128)S(1)} %collective-permute-done.4), channel_id=1, source_target_pairs={{0,1},{1,0},{2,3},{3,2},{4,5},{5,4},{6,7},{7,6},{8,9},{9,8},{10,11... | collective-permute-start | bytes 393224 | tf_op jit(solution)/shard_map/ppermute | solution.py:129
  18.5 1.3 %collective-permute-start.7 = (f32[64,256]{1,0:T(8,128)S(1)}, f32[64,256]{1,0:T(8,128)S(1)}, u32[]{:S(2)}, u32[]{:S(2)}) collective-permute-start(f32[64,256]{1,0:T(8,128)S(1)} %settle.3), channel_id=1, source_target_pairs={{0,1},{1,0},{2,3},{3,2},{4,5},{5,4},{6,7},{7,6},{8,9},{9,8},{10,11... | collective-permute-start | bytes 196616 | tf_op jit(solution)/shard_map/ppermute | solution.py:129

commit v4 on v3

--- a/solution.py
+++ b/solution.py
@@ -38,22 +38,28 @@
         copy.start()
     for copy in copies:
         copy.wait()
-    out[15:16, :] = jnp.zeros((1, out.shape[1]), jnp.float32)
+    out[7:8, :] = jnp.zeros((1, out.shape[1]), jnp.float32)
+    out[11:12, :] = jnp.zeros((1, out.shape[1]), jnp.float32)
     for part, ref in enumerate((place_at, motion_at, pull_at, change_at)):
         out[4 * part : 4 * part + 3, :] = ref[...]
     for half in range(2):
         row = slice(half, half + 1)
         at = slice(half * lanes, (half + 1) * lanes)
-        out[3:4, at] = jnp.where(level_at[row, :] <= 1, mass_at[row, :], 0.0)
-        out[7:8, at] = mass_at[row, :]
-        out[11:12, at] = level_at[row, :].astype(jnp.float32)
+        rank, heavy = level_at[row, :], mass_at[row, :]
+        out[3:4, at] = jnp.where(rank <= 1, heavy, 0.0)
+        out[15:16, at] = jnp.where(rank == 0, heavy, -heavy)
+
+
+def padded(count_all, own):
+    return -(-min(count_all, own) // 24) * 24
 
 
 def plan_kernel(devices, own, fine, mid, every, listed):
     me = lax.axis_index("stars")
     first = me * own
     count_fine, count_mid, count_all = fine.shape[0], mid.shape[0], every.shape[0]
-    order = 2 + count_all
+    room = padded(count_all, own)
+    order = 1 + room
 
     def merge(index, seen):
         star = mid[index]
@@ -63,15 +69,11 @@
 
     lax.fori_loop(0, count_mid, merge, jnp.int32(0), unroll=8)
 
-    def keep(source, start):
-        def one(index, carry):
-            listed[start + index] = source[index]
-            return carry
-
-        lax.fori_loop(0, source.shape[0], one, 0, unroll=8)
-
-    keep(fine, order)
-    keep(every, 2)
+    def keep(index, carry):
+        listed[order + index] = fine[index]
+        return carry
+
+    lax.fori_loop(0, count_fine, keep, 0, unroll=8)
 
     def locate(index, carry):
         star = listed[order + index]
@@ -91,8 +93,15 @@
         return found
 
     low = below(first)
-    listed[0] = low
-    listed[1] = below(first + own) - low
+    count = below(first + own) - low
+    listed[0] = count
+
+    def mine(index, carry):
+        star = every[jnp.minimum(low + index, count_all - 1)]
+        listed[1 + index] = jnp.where(index < count, star, -1)
+        return carry
+
+    lax.fori_loop(0, room, mine, 0, unroll=8)
 
 
 def rounds_of(devices):
@@ -240,13 +249,17 @@
             upper = field[pl.ds(pl.multiple_of(index * 16, 16), 8), halves[half]]
             lower = field[pl.ds(pl.multiple_of(index * 16 + 8, 8), 8), halves[half]]
             turned = pltpu.roll(lower, 4, 0)
-            slope = jnp.where(sub < 4, pltpu.roll(upper, 4, 0), turned)
-            bend = 0.5 * lower
-            twist = jnp.where(sub < 4, turned * (1.0 / 6.0), 0.0)
+            slope = unit * jnp.where(sub < 4, pltpu.roll(upper, 4, 0), turned)
+            bend = unit**2 * lower
+            twist = jnp.where(sub < 3, unit**3 * turned, 0.0)
+            way = slope + 0.5 * bend + twist * (1.0 / 6.0)
+            change, second = way, bend + twist
             for step in range(4):
-                time = (step + 1) * unit
-                moved = upper + time * (slope + time * (bend + time * twist))
-                ahead[step, index * 2 + half] = jnp.where(sub == 3, upper, moved)
+                ahead[step, index * 2 + half] = upper + way
+                if step < 3:
+                    change = change + second
+                    second = second + twist
+                    way = way + change
 
     together = min(4, devices)
 
@@ -256,7 +269,7 @@
             look_ahead(index * together + inner)
 
     copy.wait()
-    low, count = listed[0], listed[1]
+    count = listed[0]
 
     mine = pl.multiple_of(slot_of(me, me, devices) * 16, 16)
 
@@ -266,25 +279,26 @@
         return tile[at : at + 1, :]
 
     def fetch(block):
+        room = block if isinstance(block, int) else 0
         name = jnp.zeros((8, lanes), jnp.int32)
         for row in range(8):
-            at = 2 + count_all + block * 8 + row
+            at = 1 + padded(count_all, own_count) + block * 8 + row
             star = listed[at]
             base = pl.multiple_of(listed[at + count_mid], 16)
             side = pl.multiple_of(listed[at + 2 * count_mid], lanes)
-            slab[16 * row : 16 * row + 16, :] = field[pl.ds(base, 16), pl.ds(side, lanes)]
+            slab[room, 16 * row : 16 * row + 16, :] = field[pl.ds(base, 16), pl.ds(side, lanes)]
             name = jnp.where(sub == row, star, name)
         names[rows8(block), :] = name
         hit = (name & (lanes - 1)) == lane
         for part in range(4):
             for component in range(3):
-                value = slab[pl.ds(4 * part + component, 8, stride=16), :]
+                value = slab[room, pl.ds(4 * part + component, 8, stride=16), :]
                 table[3 * part + component, rows8(block), :] = lane_total(jnp.where(hit, value, 0.0))
-        mass = slab[pl.ds(7, 8, stride=16), :]
-        table[12, rows8(block), :] = lane_total(jnp.where(hit, mass, 0.0))
+        mass = slab[room, pl.ds(15, 8, stride=16), :]
+        table[12, rows8(block), :] = -lane_total(jnp.where(hit, mass, 0.0))
 
     loop(blocks, fetch)
-    level = [own(2, 3, half) for half in range(2)]
+    slow = [own(0, 3, half) > 0.0 for half in range(2)]
 
     def turn(ref, group, *at):
         total = jnp.zeros((8, lanes), ref.dtype)
@@ -297,7 +311,7 @@
         mid_field[group, 6:7, :] = turn(table, group, 12)
         found = turn(names, group)
         if blocks * 8 < lanes:
-            found = jnp.where(lane[0:1, :] < blocks * 8, found, -1)
+            found = jnp.where(lane[0:1, :] < blocks * 8, found, -2)
         mid_names[group, 0:1, :] = found
 
     loop(groups, fixed)
@@ -386,13 +400,12 @@
     def finish(wide, turn_at):
         hits, states, elapses, targets = [], [], [], []
         for side in range(wide):
-            name = jnp.full((8, lanes), -1, jnp.int32)
+            name = jnp.zeros((8, lanes), jnp.int32)
             for row in range(8):
-                at = (turn_at * wide + side) * 8 + row
-                star = listed[2 + jnp.minimum(low + at, count_all - 1)]
-                name = jnp.where((sub == row) & (at < count), star, name)
+                star = listed[1 + (turn_at * wide + side) * 8 + row]
+                name = jnp.where(sub == row, star, name)
             own_hit = [name == lane + (first + half * lanes) for half in range(2)]
-            coarse = [own_hit[half] & (level[half] == 1.0) for half in range(2)]
+            coarse = [own_hit[half] & slow[half] for half in range(2)]
             mid_hit = [name == mid_names[group, 0:1, :] for group in range(groups)]
 
             def find(part, component):
@@ -441,7 +454,7 @@
 
     for part, ref in enumerate((out_place, out_motion, out_pull, out_change)):
         for half in range(2):
-            changed = level[half] >= 1.0
+            changed = own(3, 3, half) < 0.0
             for index in range(3):
                 value = jnp.sum(result[part, half, index], axis=0, keepdims=True)
                 ref[index : index + 1, halves[half]] = jnp.where(
@@ -465,7 +478,7 @@
         name="pack",
     )(place, motion, pull, change, masses.reshape(2, lanes), star_level.reshape(2, lanes))
 
-    listed_shape = (2 + sizes[2] + 3 * sizes[1],)
+    listed_shape = (1 + padded(sizes[2], own_count) + 3 * sizes[1],)
 
     def plan(lists):
         return pl.pallas_call(
@@ -487,7 +500,7 @@
         out_specs=(vmem,) * 4,
         scratch_shapes=[
             pltpu.VMEM((4, devices * 2, 8, lanes), jnp.float32),
-            pltpu.VMEM((8 * 16, lanes), jnp.float32),
+            pltpu.VMEM((min(4, sizes[1] // 8), 8 * 16, lanes), jnp.float32),
             pltpu.VMEM((13, sizes[1], lanes), jnp.float32),
             pltpu.VMEM((sizes[1], lanes), jnp.int32),
             pltpu.VMEM((6, sizes[1], lanes), jnp.float32),

time: 25.8 us -> 25.9 us (level)
  Pallas kernels: 9.15 us -> 9.68 us
    pallas_call x1, Pallas kernels: 5.75 us -> 6.11 us  [body(): pl.pallas_call(functools.partial(main_kernel, devices, own_count, sizes),...]
where the time goes in v4:
time: 25.9 us
  starting transfers between devices  9.89 us (38%)
  Pallas kernels  9.68 us (37%)
  waiting for transfers between devices  5.48 us (21%)
  between operations  0.76 us (3%)
    ppermute x8, starting transfers between devices, fetch(): return lax.ppermute(value, 'stars', pairs)  9.89 us
    pallas_call x1, Pallas kernels, body(): pl.pallas_call(functools.partial(main_kernel, devices, own_count, sizes),...  6.11 us
    ppermute x8, waiting for transfers between devices, fetch(): return lax.ppermute(value, 'stars', pairs)  5.48 us
    pallas_call x1, Pallas kernels, plan(): pl.pallas_call(functools.partial(plan_kernel, devices, own_count), out_sh...  2.14 us
    pallas_call x1, Pallas kernels, body(): pl.pallas_call(pack_kernel, out_shape=jax.ShapeDtypeStruct((16, own_count...  1.42 us
  transfers between devices with their start and end apart: 8, of which 6 were waited for; matrix products, arithmetic and copies ran while one was open for 0% of the time, Pallas kernels for 8%

profile of v4, /device:TPU:0, one launch (start us, length us, event | category | flops | bytes accessed | tf_op | source)
XLA Modules:
  0.0 25.9 jit_solution(12520532482074888749)
XLA Ops:
  0.6 1.4 %pack.1 = f32[16,256]{1,0:T(8,128)} custom-call(f32[3,256]{1,0:T(4,128)} %place.1, f32[3,256]{1,0:T(4,128)} %motion.1, f32[3,256]{1,0:T(4,128)} %pull.1, f32[3,256]{1,0:T(4,128)} %change.1, f32[2,128]{1,0:T(2,128)} %bitcast.2, s32[2,128]{1,0:T(2,128)} %bitcast.3), custom_call_target="tpu_custom_call" | custom-call | tf_op jit(solution)/shard_map/pack/pallas_call | solution.py:472
  2.1 0.0 copy-start.3
  2.1 0.5 %collective-permute-start = (f32[16,256]{1,0:T(8,128)}, f32[16,256]{1,0:T(8,128)S(1)}, u32[]{:S(2)}, u32[]{:S(2)}) collective-permute-start(f32[16,256]{1,0:T(8,128)} %pack.1), channel_id=1, source_target_pairs={{0,1},{1,0},{2,3},{3,2},{4,5},{5,4},{6,7},{7,6},{8,9},{9,8},{10,11... | collective-permute-start | bytes 49160 | tf_op jit(solution)/shard_map/ppermute | solution.py:138
  2.6 1.0 %collective-permute-done = f32[16,256]{1,0:T(8,128)S(1)} collective-permute-done((f32[16,256]{1,0:T(8,128)}, f32[16,256]{1,0:T(8,128)S(1)}, u32[]{:S(2)}, u32[]{:S(2)}) %collective-permute-start) | collective-permute-done | bytes 16416 | tf_op jit(solution)/shard_map/ppermute | solution.py:138
  3.6 0.0 copy-done.3
  3.7 4.0 %collective-permute-start.1 = (f32[32,256]{1,0:T(8,128)S(1)}, f32[32,256]{1,0:T(8,128)S(1)}, u32[]{:S(2)}, u32[]{:S(2)}) collective-permute-start(f32[32,256]{1,0:T(8,128)S(1)} %pad_maximum_fusion), channel_id=1, source_target_pairs={{0,16},{1,25},{2,18},{3,27},{4,20},{5,29},{6,22},{7,31},{8,24},{9,... | collective-permute-start | bytes 98312 | tf_op jit(solution)/shard_map/ppermute | solution.py:138
  7.7 1.6 %collective-permute-start.3 = (f32[32,256]{1,0:T(8,128)S(1)}, f32[32,256]{1,0:T(8,128)S(1)}, u32[]{:S(2)}, u32[]{:S(2)}) collective-permute-start(f32[32,256]{1,0:T(8,128)S(1)} %pad_maximum_fusion), channel_id=1, source_target_pairs={{0,8},{1,9},{2,10},{3,11},{4,12},{5,13},{6,14},{7,15},{8,0},{9,1},... | collective-permute-start | bytes 98312 | tf_op jit(solution)/shard_map/ppermute | solution.py:138
  9.3 0.3 %collective-permute-done.1 = f32[32,256]{1,0:T(8,128)S(1)} collective-permute-done((f32[32,256]{1,0:T(8,128)S(1)}, f32[32,256]{1,0:T(8,128)S(1)}, u32[]{:S(2)}, u32[]{:S(2)}) %collective-permute-start.1) | collective-permute-done | bytes 32800 | tf_op jit(solution)/shard_map/ppermute | solution.py:138
  9.6 0.3 %collective-permute-start.2 = (f32[32,256]{1,0:T(8,128)S(1)}, f32[32,256]{1,0:T(8,128)S(1)}, u32[]{:S(2)}, u32[]{:S(2)}) collective-permute-start(f32[32,256]{1,0:T(8,128)S(1)} %collective-permute-done.1), channel_id=1, source_target_pairs={{0,1},{1,0},{2,3},{3,2},{4,5},{5,4},{6,7},{7,6},{8,9},{9,8},{10,11... | collective-permute-start | bytes 98312 | tf_op jit(solution)/shard_map/ppermute | solution.py:138
  9.9 2.0 %collective-permute-done.3.source = f32[32,256]{1,0:T(8,128)S(1)} collective-permute-done((f32[32,256]{1,0:T(8,128)S(1)}, f32[32,256]{1,0:T(8,128)S(1)}, u32[]{:S(2)}, u32[]{:S(2)}) %collective-permute-start.3) | collective-permute-done | bytes 32800 | tf_op jit(solution)/shard_map/ppermute | solution.py:138
  11.9 0.0 collective-permute-done.2
  11.9 0.0 copy-start
  11.9 0.0 copy-start.1
  11.9 0.0 copy-start.2
  11.9 1.6 %collective-permute-start.4 = (f32[128,256]{1,0:T(8,128)S(1)}, f32[128,256]{1,0:T(8,128)S(1)}, u32[]{:S(2)}, u32[]{:S(2)}) collective-permute-start(f32[128,256]{1,0:T(8,128)S(1)} %select_dynamic-update-slice_fusion.4), channel_id=1, source_target_pairs={{0,2},{1,7},{2,0},{3,5},{4,6},{5,3},{6,4},{7,1},{8,10},{9,15},{10,... | collective-permute-start | bytes 393224 | tf_op jit(solution)/shard_map/ppermute | solution.py:138
  13.5 1.6 %collective-permute-start.6 = (f32[64,256]{1,0:T(8,128)S(1)}, f32[64,256]{1,0:T(8,128)S(1)}, u32[]{:S(2)}, u32[]{:S(2)}) collective-permute-start(f32[64,256]{1,0:T(8,128)S(1)} %slice_select_fusion), channel_id=1, source_target_pairs={{0,4},{1,5},{2,6},{3,7},{4,0},{5,1},{6,2},{7,3},{8,12},{9,13},{10,... | collective-permute-start | bytes 196616 | tf_op jit(solution)/shard_map/ppermute | solution.py:138
  15.1 0.0 copy-done
  15.1 0.0 copy-done.1
  15.1 0.0 copy-done.2
  15.1 2.1 %plan.1.listed_from = s32[217]{0:T(256)S(1)} custom-call(s32[16]{0:T(128)S(1)} %copy-done, s32[32]{0:T(128)S(1)} %copy-done.1, s32[112]{0:T(128)S(1)} %copy-done.2), custom_call_target="tpu_custom_call" | custom-call | tf_op jit(solution)/shard_map/plan/pallas_call | solution.py:484
  17.3 1.1 %collective-permute-done.4 = f32[128,256]{1,0:T(8,128)S(1)} collective-permute-done((f32[128,256]{1,0:T(8,128)S(1)}, f32[128,256]{1,0:T(8,128)S(1)}, u32[]{:S(2)}, u32[]{:S(2)}) %collective-permute-start.4) | collective-permute-done | bytes 131104 | tf_op jit(solution)/shard_map/ppermute | solution.py:138
  18.4 0.0 collective-permute-start.5
  18.4 0.2 collective-permute-done.6.source
  18.5 0.4 %collective-permute-start.7 = (f32[64,256]{1,0:T(8,128)S(1)}, f32[64,256]{1,0:T(8,128)S(1)}, u32[]{:S(2)}, u32[]{:S(2)}) collective-permute-start(f32[64,256]{1,0:T(8,128)S(1)} %settle.3), channel_id=1, source_target_pairs={{0,1},{1,0},{2,3},{3,2},{4,5},{5,4},{6,7},{7,6},{8,9},{9,8},{10,11... | collective-permute-start | bytes 196616 | tf_op jit(solution)/shard_map/ppermute | solution.py:138
  18.9 0.8 %collective-permute-done.5 = f32[128,256]{1,0:T(8,128)S(1)} collective-permute-done((f32[128,256]{1,0:T(8,128)S(1)}, f32[128,256]{1,0:T(8,128)S(1)}, u32[]{:S(2)}, u32[]{:S(2)}) %collective-permute-start.5) | collective-permute-done | bytes 131104 | tf_op jit(solution)/shard_map/ppermute | solution.py:138
  19.8 0.0 collective-permute-done.7
  19.8 6.1 %steps.1 = (f32[3,256]{1,0:T(4,128)}, f32[3,256]{1,0:T(4,128)}, f32[3,256]{1,0:T(4,128)}, f32[3,256]{1,0:T(4,128)}) custom-call(s32[217]{0:T(256)S(1)} %plan.1.listed_from, f32[512,256]{1,0:T(8,128)S(1)} %select_dynamic-update-slice_fusion.2.field), custom_call_target="tpu_custom_call" | custom-call | tf_op jit(solution)/shard_map/steps/pallas_call | solution.py:496
  (14 shorter events, 0.1 us)
Async XLA Ops:
  2.1 1.6 %copy-start.3 = (f32[16,256]{1,0:T(8,128)S(1)}, f32[16,256]{1,0:T(8,128)}, u32[]{:S(2)}) copy-start(f32[16,256]{1,0:T(8,128)} %pack.1) | copy-start | bytes 49156
  2.1 1.6 %collective-permute-start = (f32[16,256]{1,0:T(8,128)}, f32[16,256]{1,0:T(8,128)S(1)}, u32[]{:S(2)}, u32[]{:S(2)}) collective-permute-start(f32[16,256]{1,0:T(8,128)} %pack.1), channel_id=1, source_target_pairs={{0,1},{1,0},{2,3},{3,2},{4,5},{5,4},{6,7},{7,6},{8,9},{9,8},{10,11... | collective-permute-start | bytes 49160 | tf_op jit(solution)/shard_map/ppermute | solution.py:138
  3.7 5.9 %collective-permute-start.1 = (f32[32,256]{1,0:T(8,128)S(1)}, f32[32,256]{1,0:T(8,128)S(1)}, u32[]{:S(2)}, u32[]{:S(2)}) collective-permute-start(f32[32,256]{1,0:T(8,128)S(1)} %pad_maximum_fusion), channel_id=1, source_target_pairs={{0,16},{1,25},{2,18},{3,27},{4,20},{5,29},{6,22},{7,31},{8,24},{9,... | collective-permute-start | bytes 98312 | tf_op jit(solution)/shard_map/ppermute | solution.py:138
  7.7 4.2 %collective-permute-start.3 = (f32[32,256]{1,0:T(8,128)S(1)}, f32[32,256]{1,0:T(8,128)S(1)}, u32[]{:S(2)}, u32[]{:S(2)}) collective-permute-start(f32[32,256]{1,0:T(8,128)S(1)} %pad_maximum_fusion), channel_id=1, source_target_pairs={{0,8},{1,9},{2,10},{3,11},{4,12},{5,13},{6,14},{7,15},{8,0},{9,1},... | collective-permute-start | bytes 98312 | tf_op jit(solution)/shard_map/ppermute | solution.py:138
  9.6 2.3 %collective-permute-start.2 = (f32[32,256]{1,0:T(8,128)S(1)}, f32[32,256]{1,0:T(8,128)S(1)}, u32[]{:S(2)}, u32[]{:S(2)}) collective-permute-start(f32[32,256]{1,0:T(8,128)S(1)} %collective-permute-done.1), channel_id=1, source_target_pairs={{0,1},{1,0},{2,3},{3,2},{4,5},{5,4},{6,7},{7,6},{8,9},{9,8},{10,11... | collective-permute-start | bytes 98312 | tf_op jit(solution)/shard_map/ppermute | solution.py:138
  11.9 3.2 %copy-start = (s32[16]{0:T(128)S(1)}, s32[16]{0:T(128)}, u32[]{:S(2)}) copy-start(s32[16]{0:T(128)} %fine) | copy-start | bytes 196
  11.9 3.2 %copy-start.1 = (s32[32]{0:T(128)S(1)}, s32[32]{0:T(128)}, u32[]{:S(2)}) copy-start(s32[32]{0:T(128)} %mid) | copy-start | bytes 388
  11.9 3.2 %copy-start.2 = (s32[112]{0:T(128)S(1)}, s32[112]{0:T(128)}, u32[]{:S(2)}) copy-start(s32[112]{0:T(128)} %every) | copy-start | bytes 1348
  11.9 6.4 %collective-permute-start.4 = (f32[128,256]{1,0:T(8,128)S(1)}, f32[128,256]{1,0:T(8,128)S(1)}, u32[]{:S(2)}, u32[]{:S(2)}) collective-permute-start(f32[128,256]{1,0:T(8,128)S(1)} %select_dynamic-update-slice_fusion.4), channel_id=1, source_target_pairs={{0,2},{1,7},{2,0},{3,5},{4,6},{5,3},{6,4},{7,1},{8,10},{9,15},{10,... | collective-permute-start | bytes 393224 | tf_op jit(solution)/shard_map/ppermute | solution.py:138
  13.5 5.0 %collective-permute-start.6 = (f32[64,256]{1,0:T(8,128)S(1)}, f32[64,256]{1,0:T(8,128)S(1)}, u32[]{:S(2)}, u32[]{:S(2)}) collective-permute-start(f32[64,256]{1,0:T(8,128)S(1)} %slice_select_fusion), channel_id=1, source_target_pairs={{0,4},{1,5},{2,6},{3,7},{4,0},{5,1},{6,2},{7,3},{8,12},{9,13},{10,... | collective-permute-start | bytes 196616 | tf_op jit(solution)/shard_map/ppermute | solution.py:138
  18.4 1.3 %collective-permute-start.5 = (f32[128,256]{1,0:T(8,128)S(1)}, f32[128,256]{1,0:T(8,128)S(1)}, u32[]{:S(2)}, u32[]{:S(2)}) collective-permute-start(f32[128,256]{1,0:T(8,128)S(1)} %collective-permute-done.4), channel_id=1, source_target_pairs={{0,1},{1,0},{2,3},{3,2},{4,5},{5,4},{6,7},{7,6},{8,9},{9,8},{10,11... | collective-permute-start | bytes 393224 | tf_op jit(solution)/shard_map/ppermute | solution.py:138
  18.5 1.3 %collective-permute-start.7 = (f32[64,256]{1,0:T(8,128)S(1)}, f32[64,256]{1,0:T(8,128)S(1)}, u32[]{:S(2)}, u32[]{:S(2)}) collective-permute-start(f32[64,256]{1,0:T(8,128)S(1)} %settle.3), channel_id=1, source_target_pairs={{0,1},{1,0},{2,3},{3,2},{4,5},{5,4},{6,7},{7,6},{8,9},{9,8},{10,11... | collective-permute-start | bytes 196616 | tf_op jit(solution)/shard_map/ppermute | solution.py:138

commit v5 on v4

--- a/solution.py
+++ b/solution.py
@@ -314,7 +314,8 @@
             found = jnp.where(lane[0:1, :] < blocks * 8, found, -2)
         mid_names[group, 0:1, :] = found
 
-    loop(groups, fixed)
+    def nothing():
+        pass
 
     def elapse_of(step, fine):
         return unit * (1 if fine or step % 2 == 0 else 2)
@@ -333,7 +334,7 @@
         for index in range(6):
             mid_field[group, index : index + 1, :] = turn(guess, group, index)
 
-    def force(step, targets):
+    def force(step, targets, beside):
         def add(totals, row):
             return [pair_terms(target, row, total) for target, total in zip(targets, totals)]
 
@@ -352,24 +353,36 @@
 
         zero = jnp.zeros((8, lanes), jnp.float32)
         totals = [[zero] * 6 for _ in targets]
+        most = devices // together - 1
+        totals = lax.fori_loop(0, most, some, totals)
+        beside()
+        totals = some(most, totals)
         for group in range(groups):
             totals = add(totals, [mid_field[group, k : k + 1, :] for k in range(7)])
-        totals = lax.fori_loop(0, devices // together, some, totals)
         return [[lane_total(value) for value in total] for total in totals]
 
     for step in range(4):
         loop(blocks_fine, functools.partial(guess_block, step, True))
-        loop(blocks - blocks_fine, lambda block: guess_block(step, False, block + blocks_fine))
-        loop(groups, place_mid)
+
+        def prepare(step=step):
+            if step == 0:
+                loop(groups, fixed)
+            loop(blocks - blocks_fine, lambda block: guess_block(step, False, block + blocks_fine))
+            loop(groups, place_mid)
+
         if step == 3:
             break
+        apart = blocks_fine // 2 > 4
+        if apart:
+            prepare()
 
         def advance(pair, step, fine):
             targets = [
                 [guess[index, rows8(2 * pair + side), :] for index in range(6)] for side in range(2)
             ]
             elapse = elapse_of(step, fine)
-            for side, total in enumerate(force(step, targets)):
+            early = apart or not fine or pair > 0
+            for side, total in enumerate(force(step, targets, nothing if early else prepare)):
                 rows = rows8(2 * pair + side)
                 for index in range(3):
                     moved, sped = correct(
@@ -432,7 +445,7 @@
             states.append(state)
             elapses.append(elapse)
             targets.append([pair[0] for pair in pairs] + [pair[1] for pair in pairs])
-        for side, total in enumerate(force(3, targets)):
+        for side, total in enumerate(force(3, targets, prepare)):
             for index in range(3):
                 moved, sped = correct(
                     *[states[side][part][index] for part in range(4)],

time: 25.9 us -> 25.9 us (level); the launches traced: 25.9 us -> 25.6 us
  Pallas kernels: 9.68 us -> 9.33 us
    pallas_call x1, Pallas kernels: 6.11 us -> 5.77 us  [body(): pl.pallas_call(functools.partial(main_kernel, devices, own_count, sizes),...]
where the time goes in v5:
time: 25.9 us; the launch traced here: 25.6 us
  starting transfers between devices  9.89 us (38%)
  Pallas kernels  9.33 us (36%)
  waiting for transfers between devices  5.48 us (21%)
  between operations  0.76 us (3%)
    ppermute x8, starting transfers between devices, fetch(): return lax.ppermute(value, 'stars', pairs)  9.89 us
    pallas_call x1, Pallas kernels, body(): pl.pallas_call(functools.partial(main_kernel, devices, own_count, sizes),...  5.77 us
    ppermute x8, waiting for transfers between devices, fetch(): return lax.ppermute(value, 'stars', pairs)  5.48 us
    pallas_call x1, Pallas kernels, plan(): pl.pallas_call(functools.partial(plan_kernel, devices, own_count), out_sh...  2.14 us
    pallas_call x1, Pallas kernels, body(): pl.pallas_call(pack_kernel, out_shape=jax.ShapeDtypeStruct((16, own_count...  1.42 us
  transfers between devices with their start and end apart: 8, of which 6 were waited for; matrix products, arithmetic and copies ran while one was open for 0% of the time, Pallas kernels for 8%

profile of v5, /device:TPU:0, one launch (start us, length us, event | category | flops | bytes accessed | tf_op | source)
XLA Modules:
  0.0 25.6 jit_solution(3911328488253397434)
XLA Ops:
  0.6 1.4 %pack.1 = f32[16,256]{1,0:T(8,128)} custom-call(f32[3,256]{1,0:T(4,128)} %place.1, f32[3,256]{1,0:T(4,128)} %motion.1, f32[3,256]{1,0:T(4,128)} %pull.1, f32[3,256]{1,0:T(4,128)} %change.1, f32[2,128]{1,0:T(2,128)} %bitcast.2, s32[2,128]{1,0:T(2,128)} %bitcast.3), custom_call_target="tpu_custom_call" | custom-call | tf_op jit(solution)/shard_map/pack/pallas_call | solution.py:485
  2.1 0.0 copy-start.3
  2.1 0.5 %collective-permute-start = (f32[16,256]{1,0:T(8,128)}, f32[16,256]{1,0:T(8,128)S(1)}, u32[]{:S(2)}, u32[]{:S(2)}) collective-permute-start(f32[16,256]{1,0:T(8,128)} %pack.1), channel_id=1, source_target_pairs={{0,1},{1,0},{2,3},{3,2},{4,5},{5,4},{6,7},{7,6},{8,9},{9,8},{10,11... | collective-permute-start | bytes 49160 | tf_op jit(solution)/shard_map/ppermute | solution.py:138
  2.6 1.0 %collective-permute-done = f32[16,256]{1,0:T(8,128)S(1)} collective-permute-done((f32[16,256]{1,0:T(8,128)}, f32[16,256]{1,0:T(8,128)S(1)}, u32[]{:S(2)}, u32[]{:S(2)}) %collective-permute-start) | collective-permute-done | bytes 16416 | tf_op jit(solution)/shard_map/ppermute | solution.py:138
  3.6 0.0 copy-done.3
  3.7 4.0 %collective-permute-start.1 = (f32[32,256]{1,0:T(8,128)S(1)}, f32[32,256]{1,0:T(8,128)S(1)}, u32[]{:S(2)}, u32[]{:S(2)}) collective-permute-start(f32[32,256]{1,0:T(8,128)S(1)} %pad_maximum_fusion), channel_id=1, source_target_pairs={{0,16},{1,25},{2,18},{3,27},{4,20},{5,29},{6,22},{7,31},{8,24},{9,... | collective-permute-start | bytes 98312 | tf_op jit(solution)/shard_map/ppermute | solution.py:138
  7.7 1.6 %collective-permute-start.3 = (f32[32,256]{1,0:T(8,128)S(1)}, f32[32,256]{1,0:T(8,128)S(1)}, u32[]{:S(2)}, u32[]{:S(2)}) collective-permute-start(f32[32,256]{1,0:T(8,128)S(1)} %pad_maximum_fusion), channel_id=1, source_target_pairs={{0,8},{1,9},{2,10},{3,11},{4,12},{5,13},{6,14},{7,15},{8,0},{9,1},... | collective-permute-start | bytes 98312 | tf_op jit(solution)/shard_map/ppermute | solution.py:138
  9.3 0.3 %collective-permute-done.1 = f32[32,256]{1,0:T(8,128)S(1)} collective-permute-done((f32[32,256]{1,0:T(8,128)S(1)}, f32[32,256]{1,0:T(8,128)S(1)}, u32[]{:S(2)}, u32[]{:S(2)}) %collective-permute-start.1) | collective-permute-done | bytes 32800 | tf_op jit(solution)/shard_map/ppermute | solution.py:138
  9.6 0.3 %collective-permute-start.2 = (f32[32,256]{1,0:T(8,128)S(1)}, f32[32,256]{1,0:T(8,128)S(1)}, u32[]{:S(2)}, u32[]{:S(2)}) collective-permute-start(f32[32,256]{1,0:T(8,128)S(1)} %collective-permute-done.1), channel_id=1, source_target_pairs={{0,1},{1,0},{2,3},{3,2},{4,5},{5,4},{6,7},{7,6},{8,9},{9,8},{10,11... | collective-permute-start | bytes 98312 | tf_op jit(solution)/shard_map/ppermute | solution.py:138
  9.9 2.0 %collective-permute-done.3.source = f32[32,256]{1,0:T(8,128)S(1)} collective-permute-done((f32[32,256]{1,0:T(8,128)S(1)}, f32[32,256]{1,0:T(8,128)S(1)}, u32[]{:S(2)}, u32[]{:S(2)}) %collective-permute-start.3) | collective-permute-done | bytes 32800 | tf_op jit(solution)/shard_map/ppermute | solution.py:138
  11.9 0.0 collective-permute-done.2
  11.9 0.0 copy-start
  11.9 0.0 copy-start.1
  11.9 0.0 copy-start.2
  11.9 1.6 %collective-permute-start.4 = (f32[128,256]{1,0:T(8,128)S(1)}, f32[128,256]{1,0:T(8,128)S(1)}, u32[]{:S(2)}, u32[]{:S(2)}) collective-permute-start(f32[128,256]{1,0:T(8,128)S(1)} %select_dynamic-update-slice_fusion.4), channel_id=1, source_target_pairs={{0,2},{1,7},{2,0},{3,5},{4,6},{5,3},{6,4},{7,1},{8,10},{9,15},{10,... | collective-permute-start | bytes 393224 | tf_op jit(solution)/shard_map/ppermute | solution.py:138
  13.5 1.6 %collective-permute-start.6 = (f32[64,256]{1,0:T(8,128)S(1)}, f32[64,256]{1,0:T(8,128)S(1)}, u32[]{:S(2)}, u32[]{:S(2)}) collective-permute-start(f32[64,256]{1,0:T(8,128)S(1)} %slice_select_fusion), channel_id=1, source_target_pairs={{0,4},{1,5},{2,6},{3,7},{4,0},{5,1},{6,2},{7,3},{8,12},{9,13},{10,... | collective-permute-start | bytes 196616 | tf_op jit(solution)/shard_map/ppermute | solution.py:138
  15.1 0.0 copy-done
  15.1 0.0 copy-done.1
  15.1 0.0 copy-done.2
  15.1 2.1 %plan.1.listed_from = s32[217]{0:T(256)S(1)} custom-call(s32[16]{0:T(128)S(1)} %copy-done, s32[32]{0:T(128)S(1)} %copy-done.1, s32[112]{0:T(128)S(1)} %copy-done.2), custom_call_target="tpu_custom_call" | custom-call | tf_op jit(solution)/shard_map/plan/pallas_call | solution.py:497
  17.3 1.1 %collective-permute-done.4 = f32[128,256]{1,0:T(8,128)S(1)} collective-permute-done((f32[128,256]{1,0:T(8,128)S(1)}, f32[128,256]{1,0:T(8,128)S(1)}, u32[]{:S(2)}, u32[]{:S(2)}) %collective-permute-start.4) | collective-permute-done | bytes 131104 | tf_op jit(solution)/shard_map/ppermute | solution.py:138
  18.4 0.0 collective-permute-start.5
  18.4 0.2 collective-permute-done.6.source
  18.5 0.4 %collective-permute-start.7 = (f32[64,256]{1,0:T(8,128)S(1)}, f32[64,256]{1,0:T(8,128)S(1)}, u32[]{:S(2)}, u32[]{:S(2)}) collective-permute-start(f32[64,256]{1,0:T(8,128)S(1)} %settle.3), channel_id=1, source_target_pairs={{0,1},{1,0},{2,3},{3,2},{4,5},{5,4},{6,7},{7,6},{8,9},{9,8},{10,11... | collective-permute-start | bytes 196616 | tf_op jit(solution)/shard_map/ppermute | solution.py:138
  18.9 0.8 %collective-permute-done.5 = f32[128,256]{1,0:T(8,128)S(1)} collective-permute-done((f32[128,256]{1,0:T(8,128)S(1)}, f32[128,256]{1,0:T(8,128)S(1)}, u32[]{:S(2)}, u32[]{:S(2)}) %collective-permute-start.5) | collective-permute-done | bytes 131104 | tf_op jit(solution)/shard_map/ppermute | solution.py:138
  19.8 0.0 collective-permute-done.7
  19.8 5.8 %steps.1 = (f32[3,256]{1,0:T(4,128)}, f32[3,256]{1,0:T(4,128)}, f32[3,256]{1,0:T(4,128)}, f32[3,256]{1,0:T(4,128)}) custom-call(s32[217]{0:T(256)S(1)} %plan.1.listed_from, f32[512,256]{1,0:T(8,128)S(1)} %select_dynamic-update-slice_fusion.2.field), custom_call_target="tpu_custom_call" | custom-call | tf_op jit(solution)/shard_map/steps/pallas_call | solution.py:509
  (14 shorter events, 0.1 us)
Async XLA Ops:
  2.1 1.6 %copy-start.3 = (f32[16,256]{1,0:T(8,128)S(1)}, f32[16,256]{1,0:T(8,128)}, u32[]{:S(2)}) copy-start(f32[16,256]{1,0:T(8,128)} %pack.1) | copy-start | bytes 49156
  2.1 1.6 %collective-permute-start = (f32[16,256]{1,0:T(8,128)}, f32[16,256]{1,0:T(8,128)S(1)}, u32[]{:S(2)}, u32[]{:S(2)}) collective-permute-start(f32[16,256]{1,0:T(8,128)} %pack.1), channel_id=1, source_target_pairs={{0,1},{1,0},{2,3},{3,2},{4,5},{5,4},{6,7},{7,6},{8,9},{9,8},{10,11... | collective-permute-start | bytes 49160 | tf_op jit(solution)/shard_map/ppermute | solution.py:138
  3.7 5.9 %collective-permute-start.1 = (f32[32,256]{1,0:T(8,128)S(1)}, f32[32,256]{1,0:T(8,128)S(1)}, u32[]{:S(2)}, u32[]{:S(2)}) collective-permute-start(f32[32,256]{1,0:T(8,128)S(1)} %pad_maximum_fusion), channel_id=1, source_target_pairs={{0,16},{1,25},{2,18},{3,27},{4,20},{5,29},{6,22},{7,31},{8,24},{9,... | collective-permute-start | bytes 98312 | tf_op jit(solution)/shard_map/ppermute | solution.py:138
  7.7 4.2 %collective-permute-start.3 = (f32[32,256]{1,0:T(8,128)S(1)}, f32[32,256]{1,0:T(8,128)S(1)}, u32[]{:S(2)}, u32[]{:S(2)}) collective-permute-start(f32[32,256]{1,0:T(8,128)S(1)} %pad_maximum_fusion), channel_id=1, source_target_pairs={{0,8},{1,9},{2,10},{3,11},{4,12},{5,13},{6,14},{7,15},{8,0},{9,1},... | collective-permute-start | bytes 98312 | tf_op jit(solution)/shard_map/ppermute | solution.py:138
  9.6 2.3 %collective-permute-start.2 = (f32[32,256]{1,0:T(8,128)S(1)}, f32[32,256]{1,0:T(8,128)S(1)}, u32[]{:S(2)}, u32[]{:S(2)}) collective-permute-start(f32[32,256]{1,0:T(8,128)S(1)} %collective-permute-done.1), channel_id=1, source_target_pairs={{0,1},{1,0},{2,3},{3,2},{4,5},{5,4},{6,7},{7,6},{8,9},{9,8},{10,11... | collective-permute-start | bytes 98312 | tf_op jit(solution)/shard_map/ppermute | solution.py:138
  11.9 3.2 %copy-start = (s32[16]{0:T(128)S(1)}, s32[16]{0:T(128)}, u32[]{:S(2)}) copy-start(s32[16]{0:T(128)} %fine) | copy-start | bytes 196
  11.9 3.2 %copy-start.1 = (s32[32]{0:T(128)S(1)}, s32[32]{0:T(128)}, u32[]{:S(2)}) copy-start(s32[32]{0:T(128)} %mid) | copy-start | bytes 388
  11.9 3.2 %copy-start.2 = (s32[112]{0:T(128)S(1)}, s32[112]{0:T(128)}, u32[]{:S(2)}) copy-start(s32[112]{0:T(128)} %every) | copy-start | bytes 1348
  11.9 6.4 %collective-permute-start.4 = (f32[128,256]{1,0:T(8,128)S(1)}, f32[128,256]{1,0:T(8,128)S(1)}, u32[]{:S(2)}, u32[]{:S(2)}) collective-permute-start(f32[128,256]{1,0:T(8,128)S(1)} %select_dynamic-update-slice_fusion.4), channel_id=1, source_target_pairs={{0,2},{1,7},{2,0},{3,5},{4,6},{5,3},{6,4},{7,1},{8,10},{9,15},{10,... | collective-permute-start | bytes 393224 | tf_op jit(solution)/shard_map/ppermute | solution.py:138
  13.5 5.0 %collective-permute-start.6 = (f32[64,256]{1,0:T(8,128)S(1)}, f32[64,256]{1,0:T(8,128)S(1)}, u32[]{:S(2)}, u32[]{:S(2)}) collective-permute-start(f32[64,256]{1,0:T(8,128)S(1)} %slice_select_fusion), channel_id=1, source_target_pairs={{0,4},{1,5},{2,6},{3,7},{4,0},{5,1},{6,2},{7,3},{8,12},{9,13},{10,... | collective-permute-start | bytes 196616 | tf_op jit(solution)/shard_map/ppermute | solution.py:138
  18.4 1.3 %collective-permute-start.5 = (f32[128,256]{1,0:T(8,128)S(1)}, f32[128,256]{1,0:T(8,128)S(1)}, u32[]{:S(2)}, u32[]{:S(2)}) collective-permute-start(f32[128,256]{1,0:T(8,128)S(1)} %collective-permute-done.4), channel_id=1, source_target_pairs={{0,1},{1,0},{2,3},{3,2},{4,5},{5,4},{6,7},{7,6},{8,9},{9,8},{10,11... | collective-permute-start | bytes 393224 | tf_op jit(solution)/shard_map/ppermute | solution.py:138
  18.5 1.3 %collective-permute-start.7 = (f32[64,256]{1,0:T(8,128)S(1)}, f32[64,256]{1,0:T(8,128)S(1)}, u32[]{:S(2)}, u32[]{:S(2)}) collective-permute-start(f32[64,256]{1,0:T(8,128)S(1)} %settle.3), channel_id=1, source_target_pairs={{0,1},{1,0},{2,3},{3,2},{4,5},{5,4},{6,7},{7,6},{8,9},{9,8},{10,11... | collective-permute-start | bytes 196616 | tf_op jit(solution)/shard_map/ppermute | solution.py:138

commit v6 on v5

--- a/solution.py
+++ b/solution.py
@@ -344,7 +344,7 @@
                 totals = add(totals, row)
             return totals
 
-        together = min(8, devices)
+        together = min(4, devices)
 
         def some(index, totals):
             for inner in range(together):

time: 25.9 us -> 26.3 us (1.015)
  Pallas kernels: 9.33 us -> 9.82 us
    pallas_call x1, Pallas kernels: 5.77 us -> 6.25 us  [body(): pl.pallas_call(functools.partial(main_kernel, devices, own_count, sizes),...]
where the time goes in v6:
time: 26.3 us; the launch traced here: 26.1 us
  starting transfers between devices  9.89 us (38%)
  Pallas kernels  9.82 us (37%)
  waiting for transfers between devices  5.48 us (21%)
  between operations  0.76 us (3%)
    ppermute x8, starting transfers between devices, fetch(): return lax.ppermute(value, 'stars', pairs)  9.89 us
    pallas_call x1, Pallas kernels, body(): pl.pallas_call(functools.partial(main_kernel, devices, own_count, sizes),...  6.25 us
    ppermute x8, waiting for transfers between devices, fetch(): return lax.ppermute(value, 'stars', pairs)  5.48 us
    pallas_call x1, Pallas kernels, plan(): pl.pallas_call(functools.partial(plan_kernel, devices, own_count), out_sh...  2.14 us
    pallas_call x1, Pallas kernels, body(): pl.pallas_call(pack_kernel, out_shape=jax.ShapeDtypeStruct((16, own_count...  1.42 us
  transfers between devices with their start and end apart: 8, of which 6 were waited for; matrix products, arithmetic and copies ran while one was open for 0% of the time, Pallas kernels for 8%

profile of v6, /device:TPU:0, one launch (start us, length us, event | category | flops | bytes accessed | tf_op | source)
XLA Modules:
  0.0 26.1 jit_solution(14376025648428852464)
XLA Ops:
  0.6 1.4 %pack.1 = f32[16,256]{1,0:T(8,128)} custom-call(f32[3,256]{1,0:T(4,128)} %place.1, f32[3,256]{1,0:T(4,128)} %motion.1, f32[3,256]{1,0:T(4,128)} %pull.1, f32[3,256]{1,0:T(4,128)} %change.1, f32[2,128]{1,0:T(2,128)} %bitcast.2, s32[2,128]{1,0:T(2,128)} %bitcast.3), custom_call_target="tpu_custom_call" | custom-call | tf_op jit(solution)/shard_map/pack/pallas_call | solution.py:485
  2.1 0.0 copy-start.3
  2.1 0.5 %collective-permute-start = (f32[16,256]{1,0:T(8,128)}, f32[16,256]{1,0:T(8,128)S(1)}, u32[]{:S(2)}, u32[]{:S(2)}) collective-permute-start(f32[16,256]{1,0:T(8,128)} %pack.1), channel_id=1, source_target_pairs={{0,1},{1,0},{2,3},{3,2},{4,5},{5,4},{6,7},{7,6},{8,9},{9,8},{10,11... | collective-permute-start | bytes 49160 | tf_op jit(solution)/shard_map/ppermute | solution.py:138
  2.6 1.0 %collective-permute-done = f32[16,256]{1,0:T(8,128)S(1)} collective-permute-done((f32[16,256]{1,0:T(8,128)}, f32[16,256]{1,0:T(8,128)S(1)}, u32[]{:S(2)}, u32[]{:S(2)}) %collective-permute-start) | collective-permute-done | bytes 16416 | tf_op jit(solution)/shard_map/ppermute | solution.py:138
  3.6 0.0 copy-done.3
  3.7 4.0 %collective-permute-start.1 = (f32[32,256]{1,0:T(8,128)S(1)}, f32[32,256]{1,0:T(8,128)S(1)}, u32[]{:S(2)}, u32[]{:S(2)}) collective-permute-start(f32[32,256]{1,0:T(8,128)S(1)} %pad_maximum_fusion), channel_id=1, source_target_pairs={{0,16},{1,25},{2,18},{3,27},{4,20},{5,29},{6,22},{7,31},{8,24},{9,... | collective-permute-start | bytes 98312 | tf_op jit(solution)/shard_map/ppermute | solution.py:138
  7.7 1.6 %collective-permute-start.3 = (f32[32,256]{1,0:T(8,128)S(1)}, f32[32,256]{1,0:T(8,128)S(1)}, u32[]{:S(2)}, u32[]{:S(2)}) collective-permute-start(f32[32,256]{1,0:T(8,128)S(1)} %pad_maximum_fusion), channel_id=1, source_target_pairs={{0,8},{1,9},{2,10},{3,11},{4,12},{5,13},{6,14},{7,15},{8,0},{9,1},... | collective-permute-start | bytes 98312 | tf_op jit(solution)/shard_map/ppermute | solution.py:138
  9.3 0.3 %collective-permute-done.1 = f32[32,256]{1,0:T(8,128)S(1)} collective-permute-done((f32[32,256]{1,0:T(8,128)S(1)}, f32[32,256]{1,0:T(8,128)S(1)}, u32[]{:S(2)}, u32[]{:S(2)}) %collective-permute-start.1) | collective-permute-done | bytes 32800 | tf_op jit(solution)/shard_map/ppermute | solution.py:138
  9.6 0.3 %collective-permute-start.2 = (f32[32,256]{1,0:T(8,128)S(1)}, f32[32,256]{1,0:T(8,128)S(1)}, u32[]{:S(2)}, u32[]{:S(2)}) collective-permute-start(f32[32,256]{1,0:T(8,128)S(1)} %collective-permute-done.1), channel_id=1, source_target_pairs={{0,1},{1,0},{2,3},{3,2},{4,5},{5,4},{6,7},{7,6},{8,9},{9,8},{10,11... | collective-permute-start | bytes 98312 | tf_op jit(solution)/shard_map/ppermute | solution.py:138
  9.9 2.0 %collective-permute-done.3.source = f32[32,256]{1,0:T(8,128)S(1)} collective-permute-done((f32[32,256]{1,0:T(8,128)S(1)}, f32[32,256]{1,0:T(8,128)S(1)}, u32[]{:S(2)}, u32[]{:S(2)}) %collective-permute-start.3) | collective-permute-done | bytes 32800 | tf_op jit(solution)/shard_map/ppermute | solution.py:138
  11.9 0.0 collective-permute-done.2
  11.9 0.0 copy-start
  11.9 0.0 copy-start.1
  11.9 0.0 copy-start.2
  11.9 1.6 %collective-permute-start.4 = (f32[128,256]{1,0:T(8,128)S(1)}, f32[128,256]{1,0:T(8,128)S(1)}, u32[]{:S(2)}, u32[]{:S(2)}) collective-permute-start(f32[128,256]{1,0:T(8,128)S(1)} %select_dynamic-update-slice_fusion.4), channel_id=1, source_target_pairs={{0,2},{1,7},{2,0},{3,5},{4,6},{5,3},{6,4},{7,1},{8,10},{9,15},{10,... | collective-permute-start | bytes 393224 | tf_op jit(solution)/shard_map/ppermute | solution.py:138
  13.5 1.6 %collective-permute-start.6 = (f32[64,256]{1,0:T(8,128)S(1)}, f32[64,256]{1,0:T(8,128)S(1)}, u32[]{:S(2)}, u32[]{:S(2)}) collective-permute-start(f32[64,256]{1,0:T(8,128)S(1)} %slice_select_fusion), channel_id=1, source_target_pairs={{0,4},{1,5},{2,6},{3,7},{4,0},{5,1},{6,2},{7,3},{8,12},{9,13},{10,... | collective-permute-start | bytes 196616 | tf_op jit(solution)/shard_map/ppermute | solution.py:138
  15.1 0.0 copy-done
  15.1 0.0 copy-done.1
  15.1 0.0 copy-done.2
  15.1 2.1 %plan.1.listed_from = s32[217]{0:T(256)S(1)} custom-call(s32[16]{0:T(128)S(1)} %copy-done, s32[32]{0:T(128)S(1)} %copy-done.1, s32[112]{0:T(128)S(1)} %copy-done.2), custom_call_target="tpu_custom_call" | custom-call | tf_op jit(solution)/shard_map/plan/pallas_call | solution.py:497
  17.3 1.1 %collective-permute-done.4 = f32[128,256]{1,0:T(8,128)S(1)} collective-permute-done((f32[128,256]{1,0:T(8,128)S(1)}, f32[128,256]{1,0:T(8,128)S(1)}, u32[]{:S(2)}, u32[]{:S(2)}) %collective-permute-start.4) | collective-permute-done | bytes 131104 | tf_op jit(solution)/shard_map/ppermute | solution.py:138
  18.4 0.0 collective-permute-start.5
  18.4 0.2 collective-permute-done.6.source
  18.5 0.4 %collective-permute-start.7 = (f32[64,256]{1,0:T(8,128)S(1)}, f32[64,256]{1,0:T(8,128)S(1)}, u32[]{:S(2)}, u32[]{:S(2)}) collective-permute-start(f32[64,256]{1,0:T(8,128)S(1)} %settle.3), channel_id=1, source_target_pairs={{0,1},{1,0},{2,3},{3,2},{4,5},{5,4},{6,7},{7,6},{8,9},{9,8},{10,11... | collective-permute-start | bytes 196616 | tf_op jit(solution)/shard_map/ppermute | solution.py:138
  18.9 0.8 %collective-permute-done.5 = f32[128,256]{1,0:T(8,128)S(1)} collective-permute-done((f32[128,256]{1,0:T(8,128)S(1)}, f32[128,256]{1,0:T(8,128)S(1)}, u32[]{:S(2)}, u32[]{:S(2)}) %collective-permute-start.5) | collective-permute-done | bytes 131104 | tf_op jit(solution)/shard_map/ppermute | solution.py:138
  19.8 0.0 collective-permute-done.7
  19.8 6.2 %steps.1 = (f32[3,256]{1,0:T(4,128)}, f32[3,256]{1,0:T(4,128)}, f32[3,256]{1,0:T(4,128)}, f32[3,256]{1,0:T(4,128)}) custom-call(s32[217]{0:T(256)S(1)} %plan.1.listed_from, f32[512,256]{1,0:T(8,128)S(1)} %select_dynamic-update-slice_fusion.2.field), custom_call_target="tpu_custom_call" | custom-call | tf_op jit(solution)/shard_map/steps/pallas_call | solution.py:509
  (14 shorter events, 0.1 us)
Async XLA Ops:
  2.1 1.6 %copy-start.3 = (f32[16,256]{1,0:T(8,128)S(1)}, f32[16,256]{1,0:T(8,128)}, u32[]{:S(2)}) copy-start(f32[16,256]{1,0:T(8,128)} %pack.1) | copy-start | bytes 49156
  2.1 1.6 %collective-permute-start = (f32[16,256]{1,0:T(8,128)}, f32[16,256]{1,0:T(8,128)S(1)}, u32[]{:S(2)}, u32[]{:S(2)}) collective-permute-start(f32[16,256]{1,0:T(8,128)} %pack.1), channel_id=1, source_target_pairs={{0,1},{1,0},{2,3},{3,2},{4,5},{5,4},{6,7},{7,6},{8,9},{9,8},{10,11... | collective-permute-start | bytes 49160 | tf_op jit(solution)/shard_map/ppermute | solution.py:138
  3.7 5.9 %collective-permute-start.1 = (f32[32,256]{1,0:T(8,128)S(1)}, f32[32,256]{1,0:T(8,128)S(1)}, u32[]{:S(2)}, u32[]{:S(2)}) collective-permute-start(f32[32,256]{1,0:T(8,128)S(1)} %pad_maximum_fusion), channel_id=1, source_target_pairs={{0,16},{1,25},{2,18},{3,27},{4,20},{5,29},{6,22},{7,31},{8,24},{9,... | collective-permute-start | bytes 98312 | tf_op jit(solution)/shard_map/ppermute | solution.py:138
  7.7 4.2 %collective-permute-start.3 = (f32[32,256]{1,0:T(8,128)S(1)}, f32[32,256]{1,0:T(8,128)S(1)}, u32[]{:S(2)}, u32[]{:S(2)}) collective-permute-start(f32[32,256]{1,0:T(8,128)S(1)} %pad_maximum_fusion), channel_id=1, source_target_pairs={{0,8},{1,9},{2,10},{3,11},{4,12},{5,13},{6,14},{7,15},{8,0},{9,1},... | collective-permute-start | bytes 98312 | tf_op jit(solution)/shard_map/ppermute | solution.py:138
  9.6 2.3 %collective-permute-start.2 = (f32[32,256]{1,0:T(8,128)S(1)}, f32[32,256]{1,0:T(8,128)S(1)}, u32[]{:S(2)}, u32[]{:S(2)}) collective-permute-start(f32[32,256]{1,0:T(8,128)S(1)} %collective-permute-done.1), channel_id=1, source_target_pairs={{0,1},{1,0},{2,3},{3,2},{4,5},{5,4},{6,7},{7,6},{8,9},{9,8},{10,11... | collective-permute-start | bytes 98312 | tf_op jit(solution)/shard_map/ppermute | solution.py:138
  11.9 3.2 %copy-start = (s32[16]{0:T(128)S(1)}, s32[16]{0:T(128)}, u32[]{:S(2)}) copy-start(s32[16]{0:T(128)} %fine) | copy-start | bytes 196
  11.9 3.2 %copy-start.1 = (s32[32]{0:T(128)S(1)}, s32[32]{0:T(128)}, u32[]{:S(2)}) copy-start(s32[32]{0:T(128)} %mid) | copy-start | bytes 388
  11.9 3.2 %copy-start.2 = (s32[112]{0:T(128)S(1)}, s32[112]{0:T(128)}, u32[]{:S(2)}) copy-start(s32[112]{0:T(128)} %every) | copy-start | bytes 1348
  11.9 6.4 %collective-permute-start.4 = (f32[128,256]{1,0:T(8,128)S(1)}, f32[128,256]{1,0:T(8,128)S(1)}, u32[]{:S(2)}, u32[]{:S(2)}) collective-permute-start(f32[128,256]{1,0:T(8,128)S(1)} %select_dynamic-update-slice_fusion.4), channel_id=1, source_target_pairs={{0,2},{1,7},{2,0},{3,5},{4,6},{5,3},{6,4},{7,1},{8,10},{9,15},{10,... | collective-permute-start | bytes 393224 | tf_op jit(solution)/shard_map/ppermute | solution.py:138
  13.5 5.0 %collective-permute-start.6 = (f32[64,256]{1,0:T(8,128)S(1)}, f32[64,256]{1,0:T(8,128)S(1)}, u32[]{:S(2)}, u32[]{:S(2)}) collective-permute-start(f32[64,256]{1,0:T(8,128)S(1)} %slice_select_fusion), channel_id=1, source_target_pairs={{0,4},{1,5},{2,6},{3,7},{4,0},{5,1},{6,2},{7,3},{8,12},{9,13},{10,... | collective-permute-start | bytes 196616 | tf_op jit(solution)/shard_map/ppermute | solution.py:138
  18.4 1.3 %collective-permute-start.5 = (f32[128,256]{1,0:T(8,128)S(1)}, f32[128,256]{1,0:T(8,128)S(1)}, u32[]{:S(2)}, u32[]{:S(2)}) collective-permute-start(f32[128,256]{1,0:T(8,128)S(1)} %collective-permute-done.4), channel_id=1, source_target_pairs={{0,1},{1,0},{2,3},{3,2},{4,5},{5,4},{6,7},{7,6},{8,9},{9,8},{10,11... | collective-permute-start | bytes 393224 | tf_op jit(solution)/shard_map/ppermute | solution.py:138
  18.5 1.3 %collective-permute-start.7 = (f32[64,256]{1,0:T(8,128)S(1)}, f32[64,256]{1,0:T(8,128)S(1)}, u32[]{:S(2)}, u32[]{:S(2)}) collective-permute-start(f32[64,256]{1,0:T(8,128)S(1)} %settle.3), channel_id=1, source_target_pairs={{0,1},{1,0},{2,3},{3,2},{4,5},{5,4},{6,7},{7,6},{8,9},{9,8},{10,11... | collective-permute-start | bytes 196616 | tf_op jit(solution)/shard_map/ppermute | solution.py:138

commit v7 on v6

--- a/solution.py
+++ b/solution.py
@@ -367,7 +367,11 @@
         def prepare(step=step):
             if step == 0:
                 loop(groups, fixed)
-            loop(blocks - blocks_fine, lambda block: guess_block(step, False, block + blocks_fine))
+            if step != 1 or blocks > 4:
+                loop(
+                    blocks - blocks_fine,
+                    lambda block: guess_block(step, False, block + blocks_fine),
+                )
             loop(groups, place_mid)
 
         if step == 3:
@@ -376,31 +380,45 @@
         if apart:
             prepare()
 
-        def advance(pair, step, fine):
+        def advance(start, step, kinds, early):
             targets = [
-                [guess[index, rows8(2 * pair + side), :] for index in range(6)] for side in range(2)
+                [guess[index, rows8(start + side), :] for index in range(6)]
+                for side in range(len(kinds))
             ]
-            elapse = elapse_of(step, fine)
-            early = apart or not fine or pair > 0
-            for side, total in enumerate(force(step, targets, nothing if early else prepare)):
-                rows = rows8(2 * pair + side)
+            totals = force(step, targets, nothing if early else prepare)
+            for side, (fine, total) in enumerate(zip(kinds, totals)):
+                rows = rows8(start + side)
                 for index in range(3):
                     moved, sped = correct(
                         *[table[3 * part + index, rows, :] for part in range(4)],
                         total[index],
                         total[3 + index],
-                        elapse,
+                        elapse_of(step, fine),
                     )
                     table[index, rows, :] = moved
                     table[3 + index, rows, :] = sped
                     table[6 + index, rows, :] = total[index]
                     table[9 + index, rows, :] = total[3 + index]
 
-        loop(blocks_fine // 2, functools.partial(advance, step=step, fine=True))
+        if not apart:
+            both = step == 1 and blocks <= 4
+            kinds = [block < blocks_fine for block in range(blocks if both else blocks_fine)]
+            if len(kinds) <= 4:
+                for block in range(blocks_fine, len(kinds)):
+                    guess_block(step, False, block)
+                advance(0, step, kinds, False)
+                if step == 1 and not both:
+                    loop(
+                        (blocks - blocks_fine) // 2,
+                        lambda pair: advance(blocks_fine + 2 * pair, 1, [False] * 2, True),
+                    )
+                continue
+            prepare()
+        loop(blocks_fine // 2, lambda pair: advance(2 * pair, step, [True] * 2, True))
         if step == 1:
             loop(
                 (blocks - blocks_fine) // 2,
-                lambda pair: advance(pair + blocks_fine // 2, step=1, fine=False),
+                lambda pair: advance(blocks_fine + 2 * pair, 1, [False] * 2, True),
             )
 
     def keep(group):

time: 26.3 us -> 25.8 us (0.981)
  Pallas kernels: 9.82 us -> 9.35 us
    pallas_call x1, Pallas kernels: 6.25 us -> 5.78 us  [body(): pl.pallas_call(functools.partial(main_kernel, devices, own_count, sizes),...]
where the time goes in v7:
time: 25.8 us; the launch traced here: 25.6 us
  starting transfers between devices  9.89 us (38%)
  Pallas kernels  9.35 us (36%)
  waiting for transfers between devices  5.48 us (21%)
  between operations  0.76 us (3%)
    ppermute x8, starting transfers between devices, fetch(): return lax.ppermute(value, 'stars', pairs)  9.89 us
    pallas_call x1, Pallas kernels, body(): pl.pallas_call(functools.partial(main_kernel, devices, own_count, sizes),...  5.78 us
    ppermute x8, waiting for transfers between devices, fetch(): return lax.ppermute(value, 'stars', pairs)  5.48 us
    pallas_call x1, Pallas kernels, plan(): pl.pallas_call(functools.partial(plan_kernel, devices, own_count), out_sh...  2.14 us
    pallas_call x1, Pallas kernels, body(): pl.pallas_call(pack_kernel, out_shape=jax.ShapeDtypeStruct((16, own_count...  1.42 us
  transfers between devices with their start and end apart: 8, of which 6 were waited for; matrix products, arithmetic and copies ran while one was open for 0% of the time, Pallas kernels for 8%

profile of v7, /device:TPU:0, one launch (start us, length us, event | category | flops | bytes accessed | tf_op | source)
XLA Modules:
  0.0 25.6 jit_solution(2637519764581064674)
XLA Ops:
  0.6 1.4 %pack.1 = f32[16,256]{1,0:T(8,128)} custom-call(f32[3,256]{1,0:T(4,128)} %place.1, f32[3,256]{1,0:T(4,128)} %motion.1, f32[3,256]{1,0:T(4,128)} %pull.1, f32[3,256]{1,0:T(4,128)} %change.1, f32[2,128]{1,0:T(2,128)} %bitcast.2, s32[2,128]{1,0:T(2,128)} %bitcast.3), custom_call_target="tpu_custom_call" | custom-call | tf_op jit(solution)/shard_map/pack/pallas_call | solution.py:503
  2.1 0.0 copy-start.3
  2.1 0.5 %collective-permute-start = (f32[16,256]{1,0:T(8,128)}, f32[16,256]{1,0:T(8,128)S(1)}, u32[]{:S(2)}, u32[]{:S(2)}) collective-permute-start(f32[16,256]{1,0:T(8,128)} %pack.1), channel_id=1, source_target_pairs={{0,1},{1,0},{2,3},{3,2},{4,5},{5,4},{6,7},{7,6},{8,9},{9,8},{10,11... | collective-permute-start | bytes 49160 | tf_op jit(solution)/shard_map/ppermute | solution.py:138
  2.6 1.0 %collective-permute-done = f32[16,256]{1,0:T(8,128)S(1)} collective-permute-done((f32[16,256]{1,0:T(8,128)}, f32[16,256]{1,0:T(8,128)S(1)}, u32[]{:S(2)}, u32[]{:S(2)}) %collective-permute-start) | collective-permute-done | bytes 16416 | tf_op jit(solution)/shard_map/ppermute | solution.py:138
  3.6 0.0 copy-done.3
  3.7 4.0 %collective-permute-start.1 = (f32[32,256]{1,0:T(8,128)S(1)}, f32[32,256]{1,0:T(8,128)S(1)}, u32[]{:S(2)}, u32[]{:S(2)}) collective-permute-start(f32[32,256]{1,0:T(8,128)S(1)} %pad_maximum_fusion), channel_id=1, source_target_pairs={{0,16},{1,25},{2,18},{3,27},{4,20},{5,29},{6,22},{7,31},{8,24},{9,... | collective-permute-start | bytes 98312 | tf_op jit(solution)/shard_map/ppermute | solution.py:138
  7.7 1.6 %collective-permute-start.3 = (f32[32,256]{1,0:T(8,128)S(1)}, f32[32,256]{1,0:T(8,128)S(1)}, u32[]{:S(2)}, u32[]{:S(2)}) collective-permute-start(f32[32,256]{1,0:T(8,128)S(1)} %pad_maximum_fusion), channel_id=1, source_target_pairs={{0,8},{1,9},{2,10},{3,11},{4,12},{5,13},{6,14},{7,15},{8,0},{9,1},... | collective-permute-start | bytes 98312 | tf_op jit(solution)/shard_map/ppermute | solution.py:138
  9.3 0.3 %collective-permute-done.1 = f32[32,256]{1,0:T(8,128)S(1)} collective-permute-done((f32[32,256]{1,0:T(8,128)S(1)}, f32[32,256]{1,0:T(8,128)S(1)}, u32[]{:S(2)}, u32[]{:S(2)}) %collective-permute-start.1) | collective-permute-done | bytes 32800 | tf_op jit(solution)/shard_map/ppermute | solution.py:138
  9.6 0.3 %collective-permute-start.2 = (f32[32,256]{1,0:T(8,128)S(1)}, f32[32,256]{1,0:T(8,128)S(1)}, u32[]{:S(2)}, u32[]{:S(2)}) collective-permute-start(f32[32,256]{1,0:T(8,128)S(1)} %collective-permute-done.1), channel_id=1, source_target_pairs={{0,1},{1,0},{2,3},{3,2},{4,5},{5,4},{6,7},{7,6},{8,9},{9,8},{10,11... | collective-permute-start | bytes 98312 | tf_op jit(solution)/shard_map/ppermute | solution.py:138
  9.9 2.0 %collective-permute-done.3.source = f32[32,256]{1,0:T(8,128)S(1)} collective-permute-done((f32[32,256]{1,0:T(8,128)S(1)}, f32[32,256]{1,0:T(8,128)S(1)}, u32[]{:S(2)}, u32[]{:S(2)}) %collective-permute-start.3) | collective-permute-done | bytes 32800 | tf_op jit(solution)/shard_map/ppermute | solution.py:138
  11.9 0.0 collective-permute-done.2
  11.9 0.0 copy-start
  11.9 0.0 copy-start.1
  11.9 0.0 copy-start.2
  11.9 1.6 %collective-permute-start.4 = (f32[128,256]{1,0:T(8,128)S(1)}, f32[128,256]{1,0:T(8,128)S(1)}, u32[]{:S(2)}, u32[]{:S(2)}) collective-permute-start(f32[128,256]{1,0:T(8,128)S(1)} %select_dynamic-update-slice_fusion.4), channel_id=1, source_target_pairs={{0,2},{1,7},{2,0},{3,5},{4,6},{5,3},{6,4},{7,1},{8,10},{9,15},{10,... | collective-permute-start | bytes 393224 | tf_op jit(solution)/shard_map/ppermute | solution.py:138
  13.5 1.6 %collective-permute-start.6 = (f32[64,256]{1,0:T(8,128)S(1)}, f32[64,256]{1,0:T(8,128)S(1)}, u32[]{:S(2)}, u32[]{:S(2)}) collective-permute-start(f32[64,256]{1,0:T(8,128)S(1)} %slice_select_fusion), channel_id=1, source_target_pairs={{0,4},{1,5},{2,6},{3,7},{4,0},{5,1},{6,2},{7,3},{8,12},{9,13},{10,... | collective-permute-start | bytes 196616 | tf_op jit(solution)/shard_map/ppermute | solution.py:138
  15.1 0.0 copy-done
  15.1 0.0 copy-done.1
  15.1 0.0 copy-done.2
  15.1 2.1 %plan.1.listed_from = s32[217]{0:T(256)S(1)} custom-call(s32[16]{0:T(128)S(1)} %copy-done, s32[32]{0:T(128)S(1)} %copy-done.1, s32[112]{0:T(128)S(1)} %copy-done.2), custom_call_target="tpu_custom_call" | custom-call | tf_op jit(solution)/shard_map/plan/pallas_call | solution.py:515
  17.3 1.1 %collective-permute-done.4 = f32[128,256]{1,0:T(8,128)S(1)} collective-permute-done((f32[128,256]{1,0:T(8,128)S(1)}, f32[128,256]{1,0:T(8,128)S(1)}, u32[]{:S(2)}, u32[]{:S(2)}) %collective-permute-start.4) | collective-permute-done | bytes 131104 | tf_op jit(solution)/shard_map/ppermute | solution.py:138
  18.4 0.0 collective-permute-start.5
  18.4 0.2 collective-permute-done.6.source
  18.5 0.4 %collective-permute-start.7 = (f32[64,256]{1,0:T(8,128)S(1)}, f32[64,256]{1,0:T(8,128)S(1)}, u32[]{:S(2)}, u32[]{:S(2)}) collective-permute-start(f32[64,256]{1,0:T(8,128)S(1)} %settle.3), channel_id=1, source_target_pairs={{0,1},{1,0},{2,3},{3,2},{4,5},{5,4},{6,7},{7,6},{8,9},{9,8},{10,11... | collective-permute-start | bytes 196616 | tf_op jit(solution)/shard_map/ppermute | solution.py:138
  18.9 0.8 %collective-permute-done.5 = f32[128,256]{1,0:T(8,128)S(1)} collective-permute-done((f32[128,256]{1,0:T(8,128)S(1)}, f32[128,256]{1,0:T(8,128)S(1)}, u32[]{:S(2)}, u32[]{:S(2)}) %collective-permute-start.5) | collective-permute-done | bytes 131104 | tf_op jit(solution)/shard_map/ppermute | solution.py:138
  19.8 0.0 collective-permute-done.7
  19.8 5.8 %steps.1 = (f32[3,256]{1,0:T(4,128)}, f32[3,256]{1,0:T(4,128)}, f32[3,256]{1,0:T(4,128)}, f32[3,256]{1,0:T(4,128)}) custom-call(s32[217]{0:T(256)S(1)} %plan.1.listed_from, f32[512,256]{1,0:T(8,128)S(1)} %select_dynamic-update-slice_fusion.2.field), custom_call_target="tpu_custom_call" | custom-call | tf_op jit(solution)/shard_map/steps/pallas_call | solution.py:527
  (14 shorter events, 0.1 us)
Async XLA Ops:
  2.1 1.6 %copy-start.3 = (f32[16,256]{1,0:T(8,128)S(1)}, f32[16,256]{1,0:T(8,128)}, u32[]{:S(2)}) copy-start(f32[16,256]{1,0:T(8,128)} %pack.1) | copy-start | bytes 49156
  2.1 1.6 %collective-permute-start = (f32[16,256]{1,0:T(8,128)}, f32[16,256]{1,0:T(8,128)S(1)}, u32[]{:S(2)}, u32[]{:S(2)}) collective-permute-start(f32[16,256]{1,0:T(8,128)} %pack.1), channel_id=1, source_target_pairs={{0,1},{1,0},{2,3},{3,2},{4,5},{5,4},{6,7},{7,6},{8,9},{9,8},{10,11... | collective-permute-start | bytes 49160 | tf_op jit(solution)/shard_map/ppermute | solution.py:138
  3.7 5.9 %collective-permute-start.1 = (f32[32,256]{1,0:T(8,128)S(1)}, f32[32,256]{1,0:T(8,128)S(1)}, u32[]{:S(2)}, u32[]{:S(2)}) collective-permute-start(f32[32,256]{1,0:T(8,128)S(1)} %pad_maximum_fusion), channel_id=1, source_target_pairs={{0,16},{1,25},{2,18},{3,27},{4,20},{5,29},{6,22},{7,31},{8,24},{9,... | collective-permute-start | bytes 98312 | tf_op jit(solution)/shard_map/ppermute | solution.py:138
  7.7 4.2 %collective-permute-start.3 = (f32[32,256]{1,0:T(8,128)S(1)}, f32[32,256]{1,0:T(8,128)S(1)}, u32[]{:S(2)}, u32[]{:S(2)}) collective-permute-start(f32[32,256]{1,0:T(8,128)S(1)} %pad_maximum_fusion), channel_id=1, source_target_pairs={{0,8},{1,9},{2,10},{3,11},{4,12},{5,13},{6,14},{7,15},{8,0},{9,1},... | collective-permute-start | bytes 98312 | tf_op jit(solution)/shard_map/ppermute | solution.py:138
  9.6 2.3 %collective-permute-start.2 = (f32[32,256]{1,0:T(8,128)S(1)}, f32[32,256]{1,0:T(8,128)S(1)}, u32[]{:S(2)}, u32[]{:S(2)}) collective-permute-start(f32[32,256]{1,0:T(8,128)S(1)} %collective-permute-done.1), channel_id=1, source_target_pairs={{0,1},{1,0},{2,3},{3,2},{4,5},{5,4},{6,7},{7,6},{8,9},{9,8},{10,11... | collective-permute-start | bytes 98312 | tf_op jit(solution)/shard_map/ppermute | solution.py:138
  11.9 3.2 %copy-start = (s32[16]{0:T(128)S(1)}, s32[16]{0:T(128)}, u32[]{:S(2)}) copy-start(s32[16]{0:T(128)} %fine) | copy-start | bytes 196
  11.9 3.2 %copy-start.1 = (s32[32]{0:T(128)S(1)}, s32[32]{0:T(128)}, u32[]{:S(2)}) copy-start(s32[32]{0:T(128)} %mid) | copy-start | bytes 388
  11.9 3.2 %copy-start.2 = (s32[112]{0:T(128)S(1)}, s32[112]{0:T(128)}, u32[]{:S(2)}) copy-start(s32[112]{0:T(128)} %every) | copy-start | bytes 1348
  11.9 6.4 %collective-permute-start.4 = (f32[128,256]{1,0:T(8,128)S(1)}, f32[128,256]{1,0:T(8,128)S(1)}, u32[]{:S(2)}, u32[]{:S(2)}) collective-permute-start(f32[128,256]{1,0:T(8,128)S(1)} %select_dynamic-update-slice_fusion.4), channel_id=1, source_target_pairs={{0,2},{1,7},{2,0},{3,5},{4,6},{5,3},{6,4},{7,1},{8,10},{9,15},{10,... | collective-permute-start | bytes 393224 | tf_op jit(solution)/shard_map/ppermute | solution.py:138
  13.5 5.0 %collective-permute-start.6 = (f32[64,256]{1,0:T(8,128)S(1)}, f32[64,256]{1,0:T(8,128)S(1)}, u32[]{:S(2)}, u32[]{:S(2)}) collective-permute-start(f32[64,256]{1,0:T(8,128)S(1)} %slice_select_fusion), channel_id=1, source_target_pairs={{0,4},{1,5},{2,6},{3,7},{4,0},{5,1},{6,2},{7,3},{8,12},{9,13},{10,... | collective-permute-start | bytes 196616 | tf_op jit(solution)/shard_map/ppermute | solution.py:138
  18.4 1.3 %collective-permute-start.5 = (f32[128,256]{1,0:T(8,128)S(1)}, f32[128,256]{1,0:T(8,128)S(1)}, u32[]{:S(2)}, u32[]{:S(2)}) collective-permute-start(f32[128,256]{1,0:T(8,128)S(1)} %collective-permute-done.4), channel_id=1, source_target_pairs={{0,1},{1,0},{2,3},{3,2},{4,5},{5,4},{6,7},{7,6},{8,9},{9,8},{10,11... | collective-permute-start | bytes 393224 | tf_op jit(solution)/shard_map/ppermute | solution.py:138
  18.5 1.3 %collective-permute-start.7 = (f32[64,256]{1,0:T(8,128)S(1)}, f32[64,256]{1,0:T(8,128)S(1)}, u32[]{:S(2)}, u32[]{:S(2)}) collective-permute-start(f32[64,256]{1,0:T(8,128)S(1)} %settle.3), channel_id=1, source_target_pairs={{0,1},{1,0},{2,3},{3,2},{4,5},{5,4},{6,7},{7,6},{8,9},{9,8},{10,11... | collective-permute-start | bytes 196616 | tf_op jit(solution)/shard_map/ppermute | solution.py:138

commit v8 on v7

--- a/solution.py
+++ b/solution.py
@@ -27,25 +27,15 @@
     return moved, sped
 
 
-def pack_kernel(place, motion, pull, change, mass, level, out, *held):
-    place_at, motion_at, pull_at, change_at, mass_at, level_at, arrived = held
-    sources = (place, motion, pull, change, mass, level)
-    copies = [
-        pltpu.make_async_copy(source, target, arrived.at[index])
-        for index, (source, target) in enumerate(zip(sources, held))
-    ]
-    for copy in copies:
-        copy.start()
-    for copy in copies:
-        copy.wait()
+def pack_kernel(place, motion, pull, change, mass, level, out):
     out[7:8, :] = jnp.zeros((1, out.shape[1]), jnp.float32)
     out[11:12, :] = jnp.zeros((1, out.shape[1]), jnp.float32)
-    for part, ref in enumerate((place_at, motion_at, pull_at, change_at)):
+    for part, ref in enumerate((place, motion, pull, change)):
         out[4 * part : 4 * part + 3, :] = ref[...]
     for half in range(2):
         row = slice(half, half + 1)
         at = slice(half * lanes, (half + 1) * lanes)
-        rank, heavy = level_at[row, :], mass_at[row, :]
+        rank, heavy = level[row, :], mass[row, :]
         out[3:4, at] = jnp.where(rank <= 1, heavy, 0.0)
         out[15:16, at] = jnp.where(rank == 0, heavy, -heavy)
 
@@ -498,14 +488,12 @@
     assert own_count == 2 * lanes
     sizes = (fine.shape[0], mid.shape[0], every.shape[0])
     groups = -(-sizes[1] // lanes)
-    held = [pltpu.VMEM((3, own_count), jnp.float32)] * 4
-    held += [pltpu.VMEM((2, lanes), jnp.float32), pltpu.VMEM((2, lanes), jnp.int32)]
     block = pl.pallas_call(
         pack_kernel,
         out_shape=jax.ShapeDtypeStruct((16, own_count), jnp.float32),
-        in_specs=[pl.BlockSpec(memory_space=pl.ANY)] * 6,
+        in_specs=[vmem] * 6,
         out_specs=vmem,
-        scratch_shapes=held + [pltpu.SemaphoreType.DMA((6,))],
+        compiler_params=pltpu.CompilerParams(vmem_limit_bytes=1024 * 1024),
         name="pack",
     )(place, motion, pull, change, masses.reshape(2, lanes), star_level.reshape(2, lanes))
 

time: 25.8 us -> 27.7 us (1.074)
  local copies, waits for them, and re-layouts: 0.04 us -> 3.46 us
  Pallas kernels: 9.35 us -> 7.93 us
    unnamed x10 -> x20, local copies, waits for them, and re-layouts: 0.04 us -> 3.46 us
    pallas_call x1, Pallas kernels: 1.42 us -> 0.01 us  [body(): pl.pallas_call(pack_kernel, out_shape=jax.ShapeDtypeStruct((16, own_count...]
where the time goes in v8:
time: 27.7 us; the launch traced here: 27.4 us
  starting transfers between devices  9.88 us (36%)
  Pallas kernels  7.93 us (29%)
  waiting for transfers between devices  5.28 us (19%)
  local copies, waits for them, and re-layouts  3.46 us (12%)
  between operations  0.76 us (3%)
    ppermute x8, starting transfers between devices, fetch(): return lax.ppermute(value, 'stars', pairs)  9.88 us
    pallas_call x1, Pallas kernels, body(): pl.pallas_call(functools.partial(main_kernel, devices, own_count, sizes),...  5.78 us
    ppermute x8, waiting for transfers between devices, fetch(): return lax.ppermute(value, 'stars', pairs)  5.28 us
    unnamed x20, local copies, waits for them, and re-layouts  3.46 us
    pallas_call x1, Pallas kernels, plan(): pl.pallas_call(functools.partial(plan_kernel, devices, own_count), out_sh...  2.14 us
  transfers between devices with their start and end apart: 8, of which 6 were waited for; matrix products, arithmetic and copies ran while one was open for 0% of the time, Pallas kernels for 8%

profile of v8, /device:TPU:0, one launch (start us, length us, event | category | flops | bytes accessed | tf_op | source)
XLA Modules:
  0.0 27.4 jit_solution(10137795570373094538)
XLA Ops:
  0.6 0.0 copy-start.5
  0.6 0.0 copy-start.4
  0.7 0.7 %copy-done.5 = s32[256]{0:T(256)S(1)} copy-done((s32[256]{0:T(256)S(1)}, s32[256]{0:T(256)}, u32[]{:S(2)}) %copy-start.5) | copy-done | bytes 1048
  1.3 0.0 copy-done.4
  1.3 0.0 copy-start
  1.3 0.7 %copy-done = f32[3,256]{1,0:T(4,128)S(1)} copy-done((f32[3,256]{1,0:T(4,128)S(1)}, f32[3,256]{1,0:T(4,128)}, u32[]{:S(2)}) %copy-start) | copy-done | bytes 3096
  2.0 0.0 copy-start.1
  2.0 0.7 %copy-done.1 = f32[3,256]{1,0:T(4,128)S(1)} copy-done((f32[3,256]{1,0:T(4,128)S(1)}, f32[3,256]{1,0:T(4,128)}, u32[]{:S(2)}) %copy-start.1) | copy-done | bytes 3096
  2.7 0.0 copy-start.2
  2.7 0.7 %copy-done.2 = f32[3,256]{1,0:T(4,128)S(1)} copy-done((f32[3,256]{1,0:T(4,128)S(1)}, f32[3,256]{1,0:T(4,128)}, u32[]{:S(2)}) %copy-start.2) | copy-done | bytes 3096
  3.4 0.0 copy-start.3
  3.4 0.7 %copy-done.3 = f32[3,256]{1,0:T(4,128)S(1)} copy-done((f32[3,256]{1,0:T(4,128)S(1)}, f32[3,256]{1,0:T(4,128)}, u32[]{:S(2)}) %copy-start.3) | copy-done | bytes 3096
  4.1 0.5 %collective-permute-start = (f32[16,256]{1,0:T(8,128)S(1)}, f32[16,256]{1,0:T(8,128)S(1)}, u32[]{:S(2)}, u32[]{:S(2)}) collective-permute-start(f32[16,256]{1,0:T(8,128)S(1)} %pack.1), channel_id=1, source_target_pairs={{0,1},{1,0},{2,3},{3,2},{4,5},{5,4},{6,7},{7,6},{8,9},{9,8},{10,11... | collective-permute-start | bytes 49160 | tf_op jit(solution)/shard_map/ppermute | solution.py:128
  4.6 0.8 %collective-permute-done = f32[16,256]{1,0:T(8,128)S(1)} collective-permute-done((f32[16,256]{1,0:T(8,128)S(1)}, f32[16,256]{1,0:T(8,128)S(1)}, u32[]{:S(2)}, u32[]{:S(2)}) %collective-permute-start) | collective-permute-done | bytes 16416 | tf_op jit(solution)/shard_map/ppermute | solution.py:128
  5.5 4.0 %collective-permute-start.1 = (f32[32,256]{1,0:T(8,128)S(1)}, f32[32,256]{1,0:T(8,128)S(1)}, u32[]{:S(2)}, u32[]{:S(2)}) collective-permute-start(f32[32,256]{1,0:T(8,128)S(1)} %pad_maximum_fusion), channel_id=1, source_target_pairs={{0,16},{1,25},{2,18},{3,27},{4,20},{5,29},{6,22},{7,31},{8,24},{9,... | collective-permute-start | bytes 98312 | tf_op jit(solution)/shard_map/ppermute | solution.py:128
  9.5 1.6 %collective-permute-start.3 = (f32[32,256]{1,0:T(8,128)S(1)}, f32[32,256]{1,0:T(8,128)S(1)}, u32[]{:S(2)}, u32[]{:S(2)}) collective-permute-start(f32[32,256]{1,0:T(8,128)S(1)} %pad_maximum_fusion), channel_id=1, source_target_pairs={{0,8},{1,9},{2,10},{3,11},{4,12},{5,13},{6,14},{7,15},{8,0},{9,1},... | collective-permute-start | bytes 98312 | tf_op jit(solution)/shard_map/ppermute | solution.py:128
  11.0 0.3 %collective-permute-done.1 = f32[32,256]{1,0:T(8,128)S(1)} collective-permute-done((f32[32,256]{1,0:T(8,128)S(1)}, f32[32,256]{1,0:T(8,128)S(1)}, u32[]{:S(2)}, u32[]{:S(2)}) %collective-permute-start.1) | collective-permute-done | bytes 32800 | tf_op jit(solution)/shard_map/ppermute | solution.py:128
  11.4 0.3 %collective-permute-start.2 = (f32[32,256]{1,0:T(8,128)S(1)}, f32[32,256]{1,0:T(8,128)S(1)}, u32[]{:S(2)}, u32[]{:S(2)}) collective-permute-start(f32[32,256]{1,0:T(8,128)S(1)} %collective-permute-done.1), channel_id=1, source_target_pairs={{0,1},{1,0},{2,3},{3,2},{4,5},{5,4},{6,7},{7,6},{8,9},{9,8},{10,11... | collective-permute-start | bytes 98312 | tf_op jit(solution)/shard_map/ppermute | solution.py:128
  11.7 2.0 %collective-permute-done.3.source = f32[32,256]{1,0:T(8,128)S(1)} collective-permute-done((f32[32,256]{1,0:T(8,128)S(1)}, f32[32,256]{1,0:T(8,128)S(1)}, u32[]{:S(2)}, u32[]{:S(2)}) %collective-permute-start.3) | collective-permute-done | bytes 32800 | tf_op jit(solution)/shard_map/ppermute | solution.py:128
  13.7 0.0 collective-permute-done.2
  13.7 0.0 copy-start.6
  13.7 0.0 copy-start.7
  13.7 0.0 copy-start.8
  13.7 1.6 %collective-permute-start.4 = (f32[128,256]{1,0:T(8,128)S(1)}, f32[128,256]{1,0:T(8,128)S(1)}, u32[]{:S(2)}, u32[]{:S(2)}) collective-permute-start(f32[128,256]{1,0:T(8,128)S(1)} %select_dynamic-update-slice_fusion.4), channel_id=1, source_target_pairs={{0,2},{1,7},{2,0},{3,5},{4,6},{5,3},{6,4},{7,1},{8,10},{9,15},{10,... | collective-permute-start | bytes 393224 | tf_op jit(solution)/shard_map/ppermute | solution.py:128
  15.3 1.6 %collective-permute-start.6 = (f32[64,256]{1,0:T(8,128)S(1)}, f32[64,256]{1,0:T(8,128)S(1)}, u32[]{:S(2)}, u32[]{:S(2)}) collective-permute-start(f32[64,256]{1,0:T(8,128)S(1)} %slice_select_fusion), channel_id=1, source_target_pairs={{0,4},{1,5},{2,6},{3,7},{4,0},{5,1},{6,2},{7,3},{8,12},{9,13},{10,... | collective-permute-start | bytes 196616 | tf_op jit(solution)/shard_map/ppermute | solution.py:128
  16.9 0.0 copy-done.6
  16.9 0.0 copy-done.7
  16.9 0.0 copy-done.8
  16.9 2.1 %plan.1.listed_from = s32[217]{0:T(256)S(1)} custom-call(s32[16]{0:T(128)S(1)} %copy-done.6, s32[32]{0:T(128)S(1)} %copy-done.7, s32[112]{0:T(128)S(1)} %copy-done.8), custom_call_target="tpu_custom_call" | custom-call | tf_op jit(solution)/shard_map/plan/pallas_call | solution.py:503
  19.1 1.1 %collective-permute-done.4 = f32[128,256]{1,0:T(8,128)S(1)} collective-permute-done((f32[128,256]{1,0:T(8,128)S(1)}, f32[128,256]{1,0:T(8,128)S(1)}, u32[]{:S(2)}, u32[]{:S(2)}) %collective-permute-start.4) | collective-permute-done | bytes 131104 | tf_op jit(solution)/shard_map/ppermute | solution.py:128
  20.2 0.0 collective-permute-start.5
  20.2 0.2 collective-permute-done.6.source
  20.3 0.3 %collective-permute-start.7 = (f32[64,256]{1,0:T(8,128)S(1)}, f32[64,256]{1,0:T(8,128)S(1)}, u32[]{:S(2)}, u32[]{:S(2)}) collective-permute-start(f32[64,256]{1,0:T(8,128)S(1)} %settle.3), channel_id=1, source_target_pairs={{0,1},{1,0},{2,3},{3,2},{4,5},{5,4},{6,7},{7,6},{8,9},{9,8},{10,11... | collective-permute-start | bytes 196616 | tf_op jit(solution)/shard_map/ppermute | solution.py:128
  20.7 0.8 %collective-permute-done.5 = f32[128,256]{1,0:T(8,128)S(1)} collective-permute-done((f32[128,256]{1,0:T(8,128)S(1)}, f32[128,256]{1,0:T(8,128)S(1)}, u32[]{:S(2)}, u32[]{:S(2)}) %collective-permute-start.5) | collective-permute-done | bytes 131104 | tf_op jit(solution)/shard_map/ppermute | solution.py:128
  21.5 0.0 collective-permute-done.7
  21.6 5.8 %steps.1 = (f32[3,256]{1,0:T(4,128)}, f32[3,256]{1,0:T(4,128)}, f32[3,256]{1,0:T(4,128)}, f32[3,256]{1,0:T(4,128)}) custom-call(s32[217]{0:T(256)S(1)} %plan.1.listed_from, f32[512,256]{1,0:T(8,128)S(1)} %select_dynamic-update-slice_fusion.2.field), custom_call_target="tpu_custom_call" | custom-call | tf_op jit(solution)/shard_map/steps/pallas_call | solution.py:515
  (15 shorter events, 0.1 us)
Async XLA Ops:
  0.6 0.7 %copy-start.5 = (s32[256]{0:T(256)S(1)}, s32[256]{0:T(256)}, u32[]{:S(2)}) copy-start(s32[256]{0:T(256)} %param.14) | copy-start | bytes 3076
  0.6 0.7 %copy-start.4 = (f32[256]{0:T(256)S(1)}, f32[256]{0:T(256)}, u32[]{:S(2)}) copy-start(f32[256]{0:T(256)} %param.13) | copy-start | bytes 3076
  1.3 0.7 %copy-start = (f32[3,256]{1,0:T(4,128)S(1)}, f32[3,256]{1,0:T(4,128)}, u32[]{:S(2)}) copy-start(f32[3,256]{1,0:T(4,128)} %place.1) | copy-start | bytes 9220
  2.0 0.7 %copy-start.1 = (f32[3,256]{1,0:T(4,128)S(1)}, f32[3,256]{1,0:T(4,128)}, u32[]{:S(2)}) copy-start(f32[3,256]{1,0:T(4,128)} %motion.1) | copy-start | bytes 9220
  2.7 0.7 %copy-start.2 = (f32[3,256]{1,0:T(4,128)S(1)}, f32[3,256]{1,0:T(4,128)}, u32[]{:S(2)}) copy-start(f32[3,256]{1,0:T(4,128)} %pull.1) | copy-start | bytes 9220
  3.4 0.7 %copy-start.3 = (f32[3,256]{1,0:T(4,128)S(1)}, f32[3,256]{1,0:T(4,128)}, u32[]{:S(2)}) copy-start(f32[3,256]{1,0:T(4,128)} %change.1) | copy-start | bytes 9220
  4.1 1.4 %collective-permute-start = (f32[16,256]{1,0:T(8,128)S(1)}, f32[16,256]{1,0:T(8,128)S(1)}, u32[]{:S(2)}, u32[]{:S(2)}) collective-permute-start(f32[16,256]{1,0:T(8,128)S(1)} %pack.1), channel_id=1, source_target_pairs={{0,1},{1,0},{2,3},{3,2},{4,5},{5,4},{6,7},{7,6},{8,9},{9,8},{10,11... | collective-permute-start | bytes 49160 | tf_op jit(solution)/shard_map/ppermute | solution.py:128
  5.5 5.9 %collective-permute-start.1 = (f32[32,256]{1,0:T(8,128)S(1)}, f32[32,256]{1,0:T(8,128)S(1)}, u32[]{:S(2)}, u32[]{:S(2)}) collective-permute-start(f32[32,256]{1,0:T(8,128)S(1)} %pad_maximum_fusion), channel_id=1, source_target_pairs={{0,16},{1,25},{2,18},{3,27},{4,20},{5,29},{6,22},{7,31},{8,24},{9,... | collective-permute-start | bytes 98312 | tf_op jit(solution)/shard_map/ppermute | solution.py:128
  9.5 4.2 %collective-permute-start.3 = (f32[32,256]{1,0:T(8,128)S(1)}, f32[32,256]{1,0:T(8,128)S(1)}, u32[]{:S(2)}, u32[]{:S(2)}) collective-permute-start(f32[32,256]{1,0:T(8,128)S(1)} %pad_maximum_fusion), channel_id=1, source_target_pairs={{0,8},{1,9},{2,10},{3,11},{4,12},{5,13},{6,14},{7,15},{8,0},{9,1},... | collective-permute-start | bytes 98312 | tf_op jit(solution)/shard_map/ppermute | solution.py:128
  11.4 2.3 %collective-permute-start.2 = (f32[32,256]{1,0:T(8,128)S(1)}, f32[32,256]{1,0:T(8,128)S(1)}, u32[]{:S(2)}, u32[]{:S(2)}) collective-permute-start(f32[32,256]{1,0:T(8,128)S(1)} %collective-permute-done.1), channel_id=1, source_target_pairs={{0,1},{1,0},{2,3},{3,2},{4,5},{5,4},{6,7},{7,6},{8,9},{9,8},{10,11... | collective-permute-start | bytes 98312 | tf_op jit(solution)/shard_map/ppermute | solution.py:128
  13.7 3.2 %copy-start.6 = (s32[16]{0:T(128)S(1)}, s32[16]{0:T(128)}, u32[]{:S(2)}) copy-start(s32[16]{0:T(128)} %fine) | copy-start | bytes 196
  13.7 3.2 %copy-start.7 = (s32[32]{0:T(128)S(1)}, s32[32]{0:T(128)}, u32[]{:S(2)}) copy-start(s32[32]{0:T(128)} %mid) | copy-start | bytes 388
  13.7 3.2 %copy-start.8 = (s32[112]{0:T(128)S(1)}, s32[112]{0:T(128)}, u32[]{:S(2)}) copy-start(s32[112]{0:T(128)} %every) | copy-start | bytes 1348
  13.7 6.4 %collective-permute-start.4 = (f32[128,256]{1,0:T(8,128)S(1)}, f32[128,256]{1,0:T(8,128)S(1)}, u32[]{:S(2)}, u32[]{:S(2)}) collective-permute-start(f32[128,256]{1,0:T(8,128)S(1)} %select_dynamic-update-slice_fusion.4), channel_id=1, source_target_pairs={{0,2},{1,7},{2,0},{3,5},{4,6},{5,3},{6,4},{7,1},{8,10},{9,15},{10,... | collective-permute-start | bytes 393224 | tf_op jit(solution)/shard_map/ppermute | solution.py:128
  15.3 5.0 %collective-permute-start.6 = (f32[64,256]{1,0:T(8,128)S(1)}, f32[64,256]{1,0:T(8,128)S(1)}, u32[]{:S(2)}, u32[]{:S(2)}) collective-permute-start(f32[64,256]{1,0:T(8,128)S(1)} %slice_select_fusion), channel_id=1, source_target_pairs={{0,4},{1,5},{2,6},{3,7},{4,0},{5,1},{6,2},{7,3},{8,12},{9,13},{10,... | collective-permute-start | bytes 196616 | tf_op jit(solution)/shard_map/ppermute | solution.py:128
  20.2 1.3 %collective-permute-start.5 = (f32[128,256]{1,0:T(8,128)S(1)}, f32[128,256]{1,0:T(8,128)S(1)}, u32[]{:S(2)}, u32[]{:S(2)}) collective-permute-start(f32[128,256]{1,0:T(8,128)S(1)} %collective-permute-done.4), channel_id=1, source_target_pairs={{0,1},{1,0},{2,3},{3,2},{4,5},{5,4},{6,7},{7,6},{8,9},{9,8},{10,11... | collective-permute-start | bytes 393224 | tf_op jit(solution)/shard_map/ppermute | solution.py:128
  20.3 1.3 %collective-permute-start.7 = (f32[64,256]{1,0:T(8,128)S(1)}, f32[64,256]{1,0:T(8,128)S(1)}, u32[]{:S(2)}, u32[]{:S(2)}) collective-permute-start(f32[64,256]{1,0:T(8,128)S(1)} %settle.3), channel_id=1, source_target_pairs={{0,1},{1,0},{2,3},{3,2},{4,5},{5,4},{6,7},{7,6},{8,9},{9,8},{10,11... | collective-permute-start | bytes 196616 | tf_op jit(solution)/shard_map/ppermute | solution.py:128
